TPU v7x, 256 devices: a whole 4x4x8 slice. The times are simulated.
256 devices in a mesh: gx: 8 (over y_hi, x), gy: 32 (over z, y_lo, core).
Axes of the slice: x: 4, y: 4 (y_hi: 2, y_lo: 2; y = y_hi * 2 + y_lo), z: 8, core: 2. Of those that a mesh axis runs over, the one named last changes fastest.
Arguments:
- velocity: float32 [3, 16, 1024, 4096], P(None, None, 'gx', 'gy'), may hold values from -6 to 6
- leaf_class: int32 [16, 1024, 4096], P(None, 'gx', 'gy'), may hold values from 0 to 15
- drag_table: float32 [16], replicated, may hold values from 0.05 to 0.6
Outputs:
- tendency: float32 [3, 16, 1024, 4096], P(None, None, 'gx', 'gy')
All inputs are finite; a program needn't handle non-finite values.
Results may differ from a plain program's by a relative error of at most 0.000057.
Values sent between devices are 32-bit elements; how exact they have to be, the bound alone decides.
A program may use at most 192 MiB of HBM per device.

v0:
```python
import jax
import jax.numpy as jnp
from jax import lax
from jax.sharding import PartitionSpec as P

SPACING = 2.0
VISCOSITY = 1.0


def with_halo(array, sides, width):
    for axis, dim in sides:
        devices, length = (lax.axis_size(axis), array.shape[dim])
        up = [(i, (i + 1) % devices) for i in range(devices)]
        down = [(j, i) for i, j in up]
        last = lax.slice_in_dim(array, length - width, length, axis=dim)
        leading = lax.slice_in_dim(array, 0, width, axis=dim)
        before = lax.ppermute(last, axis, up)
        after = lax.ppermute(leading, axis, down)
        array = jnp.concatenate([before, array, after], axis=dim)
    return array


def compact_sides(values, axis_dim, length, offset):

    def shifted(step):
        return lax.slice_in_dim(values, offset + step, offset + step + length, axis=axis_dim)

    center = shifted(0)
    plus_one = shifted(1)
    minus_one = shifted(-1)
    plus_two = shifted(2)
    minus_two = shifted(-2)
    first_side = 14.0 / 9.0 / (2.0 * SPACING) * (plus_one - minus_one) + 1.0 / 9.0 / (
        4.0 * SPACING
    ) * (plus_two - minus_two)
    second_side = 12.0 / 11.0 / (SPACING * SPACING) * (
        plus_one - 2.0 * center + minus_one
    ) + 3.0 / 11.0 / (4.0 * SPACING * SPACING) * (plus_two - 2.0 * center + minus_two)
    return (first_side, second_side)


def inverse_rows(length, coupling, start_row, row_count):
    positions = jnp.arange(length)
    identity = jnp.eye(length, dtype=jnp.float32)
    below_diag = jnp.where(positions > 0, coupling, 0.0).astype(jnp.float32)
    above_diag = jnp.where(positions < length - 1, coupling, 0.0).astype(jnp.float32)
    main_diag = jnp.ones((length,), jnp.float32)
    inverse_full = lax.linalg.tridiagonal_solve(below_diag, main_diag, above_diag, identity)
    return inverse_full[start_row : start_row + row_count]


def solve_along_x(inverse, sides):
    return jnp.einsum("ij,fzjy->fziy", inverse, sides, precision=lax.Precision.HIGHEST)


def solve_along_y(inverse, sides):
    return jnp.einsum("fzxj,ij->fzxi", sides, inverse, precision=lax.Precision.HIGHEST)


def banded_solves(widened, rim_cells, cells_x, cells_y):
    along_x = widened[:, :, :, rim_cells + 2 : rim_cells + 2 + cells_y]
    along_y = widened[:, :, rim_cells + 2 : rim_cells + 2 + cells_x, :]
    length_x = cells_x + 2 * rim_cells
    length_y = cells_y + 2 * rim_cells
    first_x, second_x = compact_sides(along_x, 2, length_x, 2)
    first_y, second_y = compact_sides(along_y, 3, length_y, 2)
    gradient_x = solve_along_x(inverse_rows(length_x, 1.0 / 3.0, rim_cells, cells_x), first_x)
    curvature_x = solve_along_x(inverse_rows(length_x, 2.0 / 11.0, rim_cells, cells_x), second_x)
    gradient_y = solve_along_y(inverse_rows(length_y, 1.0 / 3.0, rim_cells, cells_y), first_y)
    curvature_y = solve_along_y(inverse_rows(length_y, 2.0 / 11.0, rim_cells, cells_y), second_y)
    return (gradient_x, curvature_x, gradient_y, curvature_y)


def body(velocity, leaf_class, drag_table):
    cells_x = velocity.shape[2]
    cells_y = velocity.shape[3]
    rim_cells = min(24, cells_x - 2, cells_y - 2)
    widened = with_halo(velocity, (("gx", 2), ("gy", 3)), rim_cells + 2)
    gradient_x, curvature_x, gradient_y, curvature_y = banded_solves(
        widened, rim_cells, cells_x, cells_y
    )
    class_count = drag_table.shape[0]
    matches = leaf_class[None] == jnp.arange(class_count, dtype=jnp.int32)[:, None, None, None]
    drag_coef = jnp.sum(jnp.where(matches, drag_table[:, None, None, None], 0.0), axis=0)
    wind_speed = jnp.sqrt(jnp.sum(velocity * velocity, axis=0))
    advection = velocity[0][None] * gradient_x + velocity[1][None] * gradient_y
    return (
        -advection
        + VISCOSITY * (curvature_x + curvature_y)
        - (drag_coef * wind_speed)[None] * velocity
    )


def solution(mesh):
    return jax.shard_map(
        body,
        mesh=mesh,
        in_specs=(P(None, None, "gx", "gy"), P(None, "gx", "gy"), P()),
        out_specs=P(None, None, "gx", "gy"),
        check_vma=False,
    )
```

profile of v0, /device:TPU:1, one launch (start us, length us, event | category | flops | bytes accessed | tf_op | source)
XLA Modules:
  0.0 1101.6 jit_solution(6901552459334471612)
XLA Ops:
  14.0 328.2 %while.16 = (s32[]{:T(128)}, f32[]{:T(128)}, f32[176]{0:T(256)S(1)}, f32[5,32]{1,0:T(8,128)S(1)}, f32[5,32,176]{2,1,0:T(8,128)S(1)}, /*index=5*/f32[5,32]{1,0:T(...) while((s32[]{:T(128)}, f32[]{:T(128)}, ...), condition=%wide.region_1.2_spmd, body=%wide.region_0.1_spmd.sunk | while | flops 17025 | bytes 206633 | solution.py:48
  57.3 20.1 %subtract_divide_fusion.186 = (f32[176]{0:T(256)S(1)}, f32[176]{0:T(256)S(1)}, f32[176]{0:T(256)S(1)}, f32[176]{0:T(256)S(1)}, f32[176]{0:T(256)S(1)}, /*index=5...) fusion(f32[176]{0:T(256)S(1)} %bitcast.1865, ...), kind=kLoop, calls=%fused_computation.35.clone.1 | loop fusion | flops 16896 | bytes 46016 | tf_op jit(solution)/shard_map/while/body/eval_jaxpr/div | solution.py:48
  122.9 20.1 %subtract_divide_fusion.186 = (f32[176]{0:T(256)S(1)}, f32[176]{0:T(256)S(1)}, f32[176]{0:T(256)S(1)}, f32[176]{0:T(256)S(1)}, f32[176]{0:T(256)S(1)}, /*index=5...) fusion(f32[176]{0:T(256)S(1)} %bitcast.1865, ...), kind=kLoop, calls=%fused_computation.35.clone.1 | loop fusion | flops 16896 | bytes 46016 | tf_op jit(solution)/shard_map/while/body/eval_jaxpr/div | solution.py:48
  188.6 20.1 %subtract_divide_fusion.186 = (f32[176]{0:T(256)S(1)}, f32[176]{0:T(256)S(1)}, f32[176]{0:T(256)S(1)}, f32[176]{0:T(256)S(1)}, f32[176]{0:T(256)S(1)}, /*index=5...) fusion(f32[176]{0:T(256)S(1)} %bitcast.1865, ...), kind=kLoop, calls=%fused_computation.35.clone.1 | loop fusion | flops 16896 | bytes 46016 | tf_op jit(solution)/shard_map/while/body/eval_jaxpr/div | solution.py:48
  254.2 20.1 %subtract_divide_fusion.186 = (f32[176]{0:T(256)S(1)}, f32[176]{0:T(256)S(1)}, f32[176]{0:T(256)S(1)}, f32[176]{0:T(256)S(1)}, f32[176]{0:T(256)S(1)}, /*index=5...) fusion(f32[176]{0:T(256)S(1)} %bitcast.1865, ...), kind=kLoop, calls=%fused_computation.35.clone.1 | loop fusion | flops 16896 | bytes 46016 | tf_op jit(solution)/shard_map/while/body/eval_jaxpr/div | solution.py:48
  319.8 20.1 %subtract_divide_fusion.186 = (f32[176]{0:T(256)S(1)}, f32[176]{0:T(256)S(1)}, f32[176]{0:T(256)S(1)}, f32[176]{0:T(256)S(1)}, f32[176]{0:T(256)S(1)}, /*index=5...) fusion(f32[176]{0:T(256)S(1)} %bitcast.1865, ...), kind=kLoop, calls=%fused_computation.35.clone.1 | loop fusion | flops 16896 | bytes 46016 | tf_op jit(solution)/shard_map/while/body/eval_jaxpr/div | solution.py:48
  371.1 108.2 %while.17 = (s32[]{:T(128)}, f32[176]{0:T(256)S(1)}, f32[5,32,176]{2,1,0:T(8,128)S(1)}, f32[5,32,176]{2,1,0:T(8,128)S(1)}, f32[5,32]{1,0:T(8,128)S(1)}, /*index=...) while((s32[]{:T(128)}, f32[176]{0:T(256)S(1)}, ...), condition=%wide.region_3.4_spmd, body=%wide.region_2.3_spmd.sunk | while | flops 11298 | bytes 204313 | solution.py:48
  372.8 19.8 %multiply_subtract_fusion.128 = (f32[176]{0:T(256)S(1)}, f32[176]{0:T(256)S(1)}, f32[176]{0:T(256)S(1)}, f32[176]{0:T(256)S(1)}, f32[176]{0:T(256)S(1)}, /*index...) fusion(f32[176]{0:T(256)S(1)} %bitcast.1959, ...), kind=kLoop, calls=%fused_computation.101.clone.1 | loop fusion | flops 11264 | bytes 45888 | tf_op jit(solution)/shard_map/while/body/eval_jaxpr/sub | solution.py:48
  394.4 19.8 %multiply_subtract_fusion.128 = (f32[176]{0:T(256)S(1)}, f32[176]{0:T(256)S(1)}, f32[176]{0:T(256)S(1)}, f32[176]{0:T(256)S(1)}, f32[176]{0:T(256)S(1)}, /*index...) fusion(f32[176]{0:T(256)S(1)} %bitcast.1959, ...), kind=kLoop, calls=%fused_computation.101.clone.1 | loop fusion | flops 11264 | bytes 45888 | tf_op jit(solution)/shard_map/while/body/eval_jaxpr/sub | solution.py:48
  416.0 19.8 %multiply_subtract_fusion.128 = (f32[176]{0:T(256)S(1)}, f32[176]{0:T(256)S(1)}, f32[176]{0:T(256)S(1)}, f32[176]{0:T(256)S(1)}, f32[176]{0:T(256)S(1)}, /*index...) fusion(f32[176]{0:T(256)S(1)} %bitcast.1959, ...), kind=kLoop, calls=%fused_computation.101.clone.1 | loop fusion | flops 11264 | bytes 45888 | tf_op jit(solution)/shard_map/while/body/eval_jaxpr/sub | solution.py:48
  437.7 19.8 %multiply_subtract_fusion.128 = (f32[176]{0:T(256)S(1)}, f32[176]{0:T(256)S(1)}, f32[176]{0:T(256)S(1)}, f32[176]{0:T(256)S(1)}, f32[176]{0:T(256)S(1)}, /*index...) fusion(f32[176]{0:T(256)S(1)} %bitcast.1959, ...), kind=kLoop, calls=%fused_computation.101.clone.1 | loop fusion | flops 11264 | bytes 45888 | tf_op jit(solution)/shard_map/while/body/eval_jaxpr/sub | solution.py:48
  459.3 19.8 %multiply_subtract_fusion.128 = (f32[176]{0:T(256)S(1)}, f32[176]{0:T(256)S(1)}, f32[176]{0:T(256)S(1)}, f32[176]{0:T(256)S(1)}, f32[176]{0:T(256)S(1)}, /*index...) fusion(f32[176]{0:T(256)S(1)} %bitcast.1959, ...), kind=kLoop, calls=%fused_computation.101.clone.1 | loop fusion | flops 11264 | bytes 45888 | tf_op jit(solution)/shard_map/while/body/eval_jaxpr/sub | solution.py:48
  479.5 324.6 %while.18 = (s32[]{:T(128)}, f32[]{:T(128)}, f32[176]{0:T(256)S(1)}, f32[5,32]{1,0:T(8,128)S(1)}, f32[5,32,176]{2,1,0:T(8,128)S(1)}, /*index=5*/f32[5,32]{1,0:T(...) while((s32[]{:T(128)}, f32[]{:T(128)}, ...), condition=%wide.region_5.6_spmd, body=%wide.region_4.5_spmd.sunk | while | flops 17025 | bytes 206633 | solution.py:48
  522.5 19.9 %subtract_divide_fusion.187 = (f32[176]{0:T(256)S(1)}, f32[176]{0:T(256)S(1)}, f32[176]{0:T(256)S(1)}, f32[176]{0:T(256)S(1)}, f32[176]{0:T(256)S(1)}, /*index=5...) fusion(f32[176]{0:T(256)S(1)} %bitcast.1879, ...), kind=kLoop, calls=%fused_computation.168.clone.1 | loop fusion | flops 16896 | bytes 46016 | tf_op jit(solution)/shard_map/while/body/eval_jaxpr/div | solution.py:48
  587.4 19.9 %subtract_divide_fusion.187 = (f32[176]{0:T(256)S(1)}, f32[176]{0:T(256)S(1)}, f32[176]{0:T(256)S(1)}, f32[176]{0:T(256)S(1)}, f32[176]{0:T(256)S(1)}, /*index=5...) fusion(f32[176]{0:T(256)S(1)} %bitcast.1879, ...), kind=kLoop, calls=%fused_computation.168.clone.1 | loop fusion | flops 16896 | bytes 46016 | tf_op jit(solution)/shard_map/while/body/eval_jaxpr/div | solution.py:48
  652.3 19.9 %subtract_divide_fusion.187 = (f32[176]{0:T(256)S(1)}, f32[176]{0:T(256)S(1)}, f32[176]{0:T(256)S(1)}, f32[176]{0:T(256)S(1)}, f32[176]{0:T(256)S(1)}, /*index=5...) fusion(f32[176]{0:T(256)S(1)} %bitcast.1879, ...), kind=kLoop, calls=%fused_computation.168.clone.1 | loop fusion | flops 16896 | bytes 46016 | tf_op jit(solution)/shard_map/while/body/eval_jaxpr/div | solution.py:48
  717.2 19.9 %subtract_divide_fusion.187 = (f32[176]{0:T(256)S(1)}, f32[176]{0:T(256)S(1)}, f32[176]{0:T(256)S(1)}, f32[176]{0:T(256)S(1)}, f32[176]{0:T(256)S(1)}, /*index=5...) fusion(f32[176]{0:T(256)S(1)} %bitcast.1879, ...), kind=kLoop, calls=%fused_computation.168.clone.1 | loop fusion | flops 16896 | bytes 46016 | tf_op jit(solution)/shard_map/while/body/eval_jaxpr/div | solution.py:48
  782.2 19.9 %subtract_divide_fusion.187 = (f32[176]{0:T(256)S(1)}, f32[176]{0:T(256)S(1)}, f32[176]{0:T(256)S(1)}, f32[176]{0:T(256)S(1)}, f32[176]{0:T(256)S(1)}, /*index=5...) fusion(f32[176]{0:T(256)S(1)} %bitcast.1879, ...), kind=kLoop, calls=%fused_computation.168.clone.1 | loop fusion | flops 16896 | bytes 46016 | tf_op jit(solution)/shard_map/while/body/eval_jaxpr/div | solution.py:48
  838.1 144.5 %while.19 = (s32[]{:T(128)}, f32[176]{0:T(256)S(1)}, f32[5,32,176]{2,1,0:T(8,128)S(1)}, f32[5,32,176]{2,1,0:T(8,128)}, f32[5,32]{1,0:T(8,128)}, /*index=5*/s32[]...) while((s32[]{:T(128)}, f32[176]{0:T(256)S(1)}, ...), condition=%wide.region_7.8_spmd, body=%wide.region_6.7_spmd.sunk | while | flops 11298 | bytes 204313 | solution.py:48
  843.0 21.2 %multiply_subtract_fusion.129 = (f32[176]{0:T(256)}, f32[176]{0:T(256)S(1)}, f32[176]{0:T(256)S(1)}, f32[176]{0:T(256)S(1)}, f32[176]{0:T(256)S(1)}, /*index=5*/...) fusion(f32[176]{0:T(256)} %bitcast.1977, ...), kind=kLoop, calls=%fused_computation.234.clone.1 | loop fusion | flops 11264 | bytes 45888 | tf_op jit(solution)/shard_map/while/body/eval_jaxpr/sub | solution.py:48
  871.9 21.2 %multiply_subtract_fusion.129 = (f32[176]{0:T(256)}, f32[176]{0:T(256)S(1)}, f32[176]{0:T(256)S(1)}, f32[176]{0:T(256)S(1)}, f32[176]{0:T(256)S(1)}, /*index=5*/...) fusion(f32[176]{0:T(256)} %bitcast.1977, ...), kind=kLoop, calls=%fused_computation.234.clone.1 | loop fusion | flops 11264 | bytes 45888 | tf_op jit(solution)/shard_map/while/body/eval_jaxpr/sub | solution.py:48
  900.8 21.2 %multiply_subtract_fusion.129 = (f32[176]{0:T(256)}, f32[176]{0:T(256)S(1)}, f32[176]{0:T(256)S(1)}, f32[176]{0:T(256)S(1)}, f32[176]{0:T(256)S(1)}, /*index=5*/...) fusion(f32[176]{0:T(256)} %bitcast.1977, ...), kind=kLoop, calls=%fused_computation.234.clone.1 | loop fusion | flops 11264 | bytes 45888 | tf_op jit(solution)/shard_map/while/body/eval_jaxpr/sub | solution.py:48
  929.7 21.2 %multiply_subtract_fusion.129 = (f32[176]{0:T(256)}, f32[176]{0:T(256)S(1)}, f32[176]{0:T(256)S(1)}, f32[176]{0:T(256)S(1)}, f32[176]{0:T(256)S(1)}, /*index=5*/...) fusion(f32[176]{0:T(256)} %bitcast.1977, ...), kind=kLoop, calls=%fused_computation.234.clone.1 | loop fusion | flops 11264 | bytes 45888 | tf_op jit(solution)/shard_map/while/body/eval_jaxpr/sub | solution.py:48
  958.6 21.2 %multiply_subtract_fusion.129 = (f32[176]{0:T(256)}, f32[176]{0:T(256)S(1)}, f32[176]{0:T(256)S(1)}, f32[176]{0:T(256)S(1)}, f32[176]{0:T(256)S(1)}, /*index=5*/...) fusion(f32[176]{0:T(256)} %bitcast.1977, ...), kind=kLoop, calls=%fused_computation.234.clone.1 | loop fusion | flops 11264 | bytes 45888 | tf_op jit(solution)/shard_map/while/body/eval_jaxpr/sub | solution.py:48
  (302 shorter events, 244.9 us)
Async XLA Ops:
  2.8 1000.3 %collective-permute-start = (f32[3,16,26,128]{3,1,2,0:T(8,128)}, f32[3,16,26,128]{3,1,2,0:T(8,128)}, u32[]{:S(2)}, u32[]{:S(2)}) collective-permute-start(f32[3,16,26,128]{3,1,2,0:T(8,128)} %copy.64), channel_id=1, source_target_pairs={{0,32},{32,64},{64,96},{96,128},{128,160},{160,192},{192,224},{224... | collective-permute-start | bytes 1916936 | tf_op jit(solution)/shard_map/ppermute | solution.py:17
  6.1 1000.2 %collective-permute-start.1 = (f32[3,16,26,128]{3,1,2,0:T(8,128)}, f32[3,16,26,128]{3,1,2,0:T(8,128)}, u32[]{:S(2)}, u32[]{:S(2)}) collective-permute-start(f32[3,16,26,128]{3,1,2,0:T(8,128)} %copy.65), channel_id=1, source_target_pairs={{32,0},{64,32},{96,64},{128,96},{160,128},{192,160},{224,192},{0,2... | collective-permute-start | bytes 1916936 | tf_op jit(solution)/shard_map/ppermute | solution.py:18
  10.5 359.5 %copy-start.10 = (f32[1,176]{1,0:T(1,128)}, f32[1,176]{1,0:T(1,128)S(1)}, u32[]{:S(2)}) copy-start(f32[1,176]{1,0:T(1,128)S(1)} %get-tuple-element.918) | copy-start | bytes 2116
  10.5 359.5 %copy-start.11 = (f32[1,176]{1,0:T(1,128)}, f32[1,176]{1,0:T(1,128)S(1)}, u32[]{:S(2)}) copy-start(f32[1,176]{1,0:T(1,128)S(1)} %get-tuple-element.919) | copy-start | bytes 2116
  10.6 359.5 %copy-start.12 = (f32[1,176]{1,0:T(1,128)}, f32[1,176]{1,0:T(1,128)S(1)}, u32[]{:S(2)}) copy-start(f32[1,176]{1,0:T(1,128)S(1)} %get-tuple-element.920) | copy-start | bytes 2116
  10.6 359.5 %copy-start.13 = (f32[1,176]{1,0:T(1,128)}, f32[1,176]{1,0:T(1,128)S(1)}, u32[]{:S(2)}) copy-start(f32[1,176]{1,0:T(1,128)S(1)} %get-tuple-element.921) | copy-start | bytes 2116
  10.6 359.5 %copy-start.14 = (f32[1,176]{1,0:T(1,128)}, f32[1,176]{1,0:T(1,128)S(1)}, u32[]{:S(2)}) copy-start(f32[1,176]{1,0:T(1,128)S(1)} %get-tuple-element.922) | copy-start | bytes 2116
  804.1 29.5 %copy-start.9 = (f32[5,32,176]{2,1,0:T(8,128)}, f32[5,32,176]{2,1,0:T(8,128)S(1)}, u32[]{:S(2)}) copy-start(f32[5,32,176]{2,1,0:T(8,128)S(1)} %get-tuple-element.360) | copy-start | bytes 337924
  804.1 182.6 %copy-start = (f32[3,16,128,128]{3,2,1,0:T(8,128)S(1)}, f32[3,16,128,128]{3,2,1,0:T(8,128)}, u32[]{:S(2)}) copy-start(f32[3,16,128,128]{3,2,1,0:T(8,128)} %param.11) | copy-start | bytes 9437188
  997.9 1.2 copy-start.7
  1000.4 9.2 copy-start.1
  1025.2 30.6 %collective-permute-start.2 = (f32[3,16,180,26]{2,1,3,0:T(8,128)}, f32[3,16,180,26]{2,1,3,0:T(8,128)S(1)}, u32[]{:S(2)}, u32[]{:S(2)}) collective-permute-start(f32[3,16,180,26]{2,1,3,0:T(8,128)} %get-tuple-element.899), channel_id=1, source_target_pairs={{0,1},{1,2},{2,3},{3,4},{4,5},{5,6},{6,7},{7,8},{8,9},{9,10},{10,1... | collective-permute-start | bytes 2695688 | tf_op jit(solution)/shard_map/ppermute | solution.py:17
  1027.6 30.6 %collective-permute-start.3 = (f32[3,16,180,26]{2,1,3,0:T(8,128)}, f32[3,16,180,26]{2,1,3,0:T(8,128)S(1)}, u32[]{:S(2)}, u32[]{:S(2)}) collective-permute-start(f32[3,16,180,26]{2,1,3,0:T(8,128)} %get-tuple-element.900), channel_id=1, source_target_pairs={{1,0},{2,1},{3,2},{4,3},{5,4},{6,5},{7,6},{8,7},{9,8},{10,9},{11,1... | collective-permute-start | bytes 2695688 | tf_op jit(solution)/shard_map/ppermute | solution.py:18
  1040.3 17.8 %copy-start.2 = (f32[3,16,128,128]{2,1,3,0:T(8,128)S(1)}, f32[3,16,128,128]{2,1,3,0:T(8,128)}, u32[]{:S(2)}) copy-start(f32[3,16,128,128]{2,1,3,0:T(8,128)} %copy.46) | copy-start | bytes 9437188
  1040.4 17.8 %copy-start.3 = (f32[3,16,26,128]{2,1,3,0:T(8,128)S(1)}, f32[3,16,26,128]{2,1,3,0:T(8,128)}, u32[]{:S(2)}) copy-start(f32[3,16,26,128]{2,1,3,0:T(8,128)} %copy.45) | copy-start | bytes 1916932
  1040.4 17.8 %copy-start.4 = (f32[3,16,26,128]{2,1,3,0:T(8,128)S(1)}, f32[3,16,26,128]{2,1,3,0:T(8,128)}, u32[]{:S(2)}) copy-start(f32[3,16,26,128]{2,1,3,0:T(8,128)} %copy.47) | copy-start | bytes 1916932
  1082.6 6.1 copy-start.5
  1082.6 6.1 copy-start.6
  1082.6 6.1 copy-start.8
where the time goes:
time: 1120 us; the launch traced here: 1100 us
  other arithmetic  469 us (42%)
  loops' own time  413 us (37%)
  local copies, waits for them, and re-layouts  127 us (11%)
  between operations  38 us (3%)
  matrix products  37.3 us (3%)
    another operation x4, loops' own time, inverse_rows(): lax.linalg.tridiagonal_solve(below_diag, main_diag, above_diag, identity)  413 us
    div x12, other arithmetic, inverse_rows(): lax.linalg.tridiagonal_solve(below_diag, main_diag, above_diag, identity)  220 us
    sub x10, other arithmetic, inverse_rows(): lax.linalg.tridiagonal_solve(below_diag, main_diag, above_diag, identity)  205 us
    slice x114, local copies, waits for them, and re-layouts, inverse_rows(): lax.linalg.tridiagonal_solve(below_diag, main_diag, above_diag, identity)  63.8 us
    concatenate x34, local copies, waits for them, and re-layouts, inverse_rows(): lax.linalg.tridiagonal_solve(below_diag, main_diag, above_diag, identity)  23.7 us
  transfers between devices with their start and end apart: 4, of which 2 were waited for; matrix products, arithmetic and copies ran while one was open for 52% of the time, Pallas kernels for 0%

commit v1 on v0

v1 whole, which is shorter than its diff:
```python
import math

import jax
import jax.numpy as jnp
import ml_dtypes
import numpy as np
from jax import lax
from jax.experimental import pallas as pl
from jax.experimental.pallas import tpu as pltpu
from jax.sharding import PartitionSpec as P

SPACING = 2.0
CELLS = 128
GROUP = 4
EDGE = 24
BF16 = jnp.bfloat16


def kernel_of(coupling, stencil):
    root = (-1.0 + math.sqrt(1.0 - 4.0 * coupling * coupling)) / (2.0 * coupling)
    scale = 1.0 / math.sqrt(1.0 - 4.0 * coupling * coupling)

    def at(d):
        return sum(w * scale * root ** abs(d - m) for m, w in stencil.items())

    amplitude = at(2) / root**2
    return at, root, amplitude


def operators():
    h = SPACING
    a, b = 14.0 / 9.0 / (2.0 * h), 1.0 / 9.0 / (4.0 * h)
    first = {-1: a, 1: -a, -2: b, 2: -b}
    c, e = 12.0 / 11.0 / (h * h), 3.0 / 11.0 / (4.0 * h * h)
    second = {-1: c, 1: c, -2: e, 2: e, 0: -2.0 * c - 2.0 * e}
    return kernel_of(1.0 / 3.0, first), kernel_of(2.0 / 11.0, second)


def split(values):
    high = np.asarray(values, np.float64).astype(ml_dtypes.bfloat16)
    low = (np.asarray(values, np.float64) - high.astype(np.float64)).astype(ml_dtypes.bfloat16)
    return high, low


def constants():
    (k1, r1, a1), (k2, r2, a2) = operators()
    n = CELLS
    d1 = np.array([[k1(i - j) for j in range(n)] for i in range(n)])
    d2 = np.array([[k2(i - j) for j in range(n)] for i in range(n)])
    rows = np.concatenate([d1.reshape(n // 8, 8, n), d2.reshape(n // 8, 8, n)], axis=1).reshape(2 * n, n)
    high, low = split(rows)
    along_x = np.concatenate([high, high, low], axis=1)
    high, low = split(np.concatenate([d1.T, d2.T], axis=1))
    i = np.arange(n)
    e1, e2 = k1(1) - a1 * r1, k2(1) - a2 * r2
    zero = np.zeros(n)
    first, last = (i == 0) * 1.0, (i == n - 1) * 1.0
    before = np.stack([
        np.concatenate([r1**i, zero]),
        np.concatenate([zero, r2**i]),
        np.concatenate([e1 * first, e2 * first]),
        np.zeros(2 * n),
    ])
    after = np.stack([
        np.concatenate([-(r1 ** (n - 1 - i)), zero]),
        np.concatenate([zero, r2 ** (n - 1 - i)]),
        np.concatenate([-e1 * last, e2 * last]),
        np.zeros(2 * n),
    ])
    spread = np.repeat(np.concatenate([before, after]), GROUP, axis=0)
    spread_high, spread_low = split(spread)
    along_y = np.concatenate([high, high, low, spread_high, spread_high, spread_low], axis=0)
    forward = np.stack([a1 * r1 ** (n - i.astype(float)), a2 * r2 ** (n - i.astype(float)), last, zero])
    backward = np.stack([a1 * r1 ** (1.0 + i), a2 * r2 ** (1.0 + i), first, zero])
    high, low = split(np.concatenate([forward, backward]))
    sums_y = np.concatenate(
        [np.concatenate([high, high], axis=1), np.concatenate([low, np.zeros_like(low)], axis=1)], axis=0
    )
    lanes = np.ones((1, n))
    edge_x = np.stack([
        forward[0, n - EDGE :, None] * lanes,
        forward[1, n - EDGE :, None] * lanes,
        backward[0, :EDGE, None] * lanes,
        backward[1, :EDGE, None] * lanes,
        (r1 ** i[:EDGE])[:, None] * lanes,
        (r2 ** i[:EDGE])[:, None] * lanes,
        (e1 * first)[:EDGE, None] * lanes,
        (e2 * first)[:EDGE, None] * lanes,
        (-(r1 ** (n - 1 - i)))[n - EDGE :, None] * lanes,
        (r2 ** (n - 1 - i))[n - EDGE :, None] * lanes,
        (-e1 * last)[n - EDGE :, None] * lanes,
        (e2 * last)[n - EDGE :, None] * lanes,
    ]).astype(np.float32)
    return along_x, along_y, sums_y, edge_x


def dot(a, b):
    return lax.dot_general(a, b, (((1,), (0,)), ((), ())), preferred_element_type=jnp.float32)


def dot_transposed(a, b):
    return lax.dot_general(a, b, (((1,), (1,)), ((), ())), preferred_element_type=jnp.float32)


def kernel(
    groups, vel_hbm, leaf_hbm, table_ref, along_x_ref, along_y_ref, sums_y_ref, edge_x_ref, out_hbm,
    vel, parts, leaf, tend, send_x, send_y, recv_x, recv_y,
    vel_sem, leaf_sem, out_sem, send_sem, recv_sem,
):
    n = CELLS

    def levels(g):
        return pl.ds(g * GROUP, GROUP)

    def vel_copy(g):
        return pltpu.make_async_copy(vel_hbm.at[:, levels(g)], vel.at[:, levels(g)], vel_sem.at[g])

    def leaf_copy(g):
        return pltpu.make_async_copy(leaf_hbm.at[levels(g)], leaf.at[levels(g)], leaf_sem.at[g])

    def out_copy(g):
        return pltpu.make_async_copy(tend.at[:, levels(g)], out_hbm.at[:, levels(g)], out_sem.at[g])

    for g in range(groups):
        vel_copy(g).start()
    for g in range(groups):
        leaf_copy(g).start()

    mx, my = lax.axis_index("gx"), lax.axis_index("gy")
    nx, ny = lax.axis_size("gx"), lax.axis_size("gy")
    targets = [
        {"gx": lax.rem(mx + 1, nx)},
        {"gx": lax.rem(mx + nx - 1, nx)},
        {"gy": lax.rem(my + 1, ny)},
        {"gy": lax.rem(my + ny - 1, ny)},
    ]
    barrier = pltpu.get_barrier_semaphore()
    for target in targets:
        pl.semaphore_signal(barrier, inc=1, device_id=target, device_id_type=pl.DeviceIdType.MESH)

    blank = jnp.zeros((GROUP, n), jnp.float32)

    @pl.loop(0, groups)
    def _(g):
        vel_copy(g).wait()
        for c in range(3):
            for k in range(GROUP):
                values = vel[c, g * GROUP + k]
                high = values.astype(BF16)
                low = (values - high.astype(jnp.float32)).astype(BF16)
                parts[c, g * GROUP + k, :, :n] = high
                parts[c, g * GROUP + k, :, n:] = low
                top, bottom = values[:EDGE], values[n - EDGE :]
                for q in range(2):
                    row = q * GROUP + k
                    send_x[0, c, g, row : row + 1] = jnp.sum(edge_x_ref[q] * bottom, axis=0, keepdims=True)
                    send_x[1, c, g, row : row + 1] = jnp.sum(edge_x_ref[2 + q] * top, axis=0, keepdims=True)
                row = 2 * GROUP + k
                send_x[0, c, g, row : row + 1] = values[n - 1 :]
                send_x[1, c, g, row : row + 1] = values[:1]
            for k in range(0, GROUP, 2):
                pair = parts[c, pl.ds(g * GROUP + k, 2)].reshape(2 * n, 2 * n)
                sums = dot_transposed(sums_y_ref[...], pair)
                sums = sums[:8] + sums[8:]
                for j in range(2):
                    for q in range(3):
                        row = q * GROUP + k + j
                        send_y[0, c, g, row : row + 1] = sums[q : q + 1, j * n : (j + 1) * n]
                        send_y[1, c, g, row : row + 1] = sums[4 + q : 5 + q, j * n : (j + 1) * n]
            for side in range(2):
                send_x[side, c, g, 3 * GROUP :] = blank
                send_y[side, c, g, 3 * GROUP :] = blank

    pl.semaphore_wait(barrier, 4)
    copies = []
    for t, target in enumerate(targets):
        source, landing = ((send_x, recv_x), (send_y, recv_y))[t // 2]
        copies.append(
            pltpu.make_async_remote_copy(
                src_ref=source.at[t % 2],
                dst_ref=landing.at[t % 2],
                send_sem=send_sem.at[t],
                recv_sem=recv_sem.at[t],
                device_id=target,
                device_id_type=pl.DeviceIdType.MESH,
            )
        )
        copies[-1].start()

    lane = lax.broadcasted_iota(jnp.int32, (n, n), 1)
    table = jnp.zeros((n, n), jnp.float32)
    for k in range(table_ref.shape[0]):
        table = jnp.where(lane == k, table_ref[k], table)

    @pl.loop(0, groups)
    def _(g):
        leaf_copy(g).wait()
        for k in range(0, GROUP, 2):
            z = (g * GROUP + k, g * GROUP + k + 1)
            drag = []
            for j in range(2):
                speed = jnp.sqrt(vel[0, z[j]] ** 2 + vel[1, z[j]] ** 2 + vel[2, z[j]] ** 2)
                drag.append(jnp.take_along_axis(table, leaf[z[j]], axis=1) * speed)
            for c in range(3):
                high = jnp.concatenate([parts[c, z[0], :, :n], parts[c, z[1], :, :n]], axis=1)
                low = jnp.concatenate([parts[c, z[0], :, n:], parts[c, z[1], :, n:]], axis=1)
                both = dot(along_x_ref[...], jnp.concatenate([high, low, high], axis=0))
                both = both.reshape(n // 8, 2, 8, 2 * n)
                for j in range(2):
                    gradient = both[:, 0, :, j * n : (j + 1) * n].reshape(n, n)
                    curvature = both[:, 1, :, j * n : (j + 1) * n].reshape(n, n)
                    tend[c, z[j]] = curvature - vel[0, z[j]] * gradient - drag[j] * vel[c, z[j]]

    for copy in copies:
        copy.wait()

    lane = lax.broadcasted_iota(jnp.int32, (n, 6 * GROUP * 4), 1)

    @pl.loop(0, groups)
    def _(g):
        spread = []
        for c in range(3):
            got = jnp.concatenate([recv_y[0, c, g], recv_y[1, c, g]], axis=0)
            high = got.astype(BF16).astype(jnp.float32)
            low = (got - high).astype(BF16).astype(jnp.float32)
            spread.append(jnp.concatenate([high, low, high], axis=0).T.astype(BF16))
        for k in range(GROUP):
            z = g * GROUP + k
            mask = (lane[:, : 24 * GROUP] % GROUP) == k
            left = []
            for c in range(3):
                mine = jnp.where(mask, spread[c], jnp.zeros_like(spread[c]))
                left.append(jnp.concatenate([parts[c, z], parts[c, z, :, :n], mine], axis=1))
            both = dot(jnp.concatenate(left, axis=0), along_y_ref[...])
            for c in range(3):
                gradient = both[c * n : (c + 1) * n, :n]
                curvature = both[c * n : (c + 1) * n, n:]
                tend[c, z] += curvature - vel[1, z] * gradient
                for side in range(2):
                    rows = pl.ds(0, EDGE) if side == 0 else pl.ds(n - EDGE, EDGE)
                    s1 = recv_x[side, c, g, k : k + 1]
                    s2 = recv_x[side, c, g, GROUP + k : GROUP + k + 1]
                    s3 = recv_x[side, c, g, 2 * GROUP + k : 2 * GROUP + k + 1]
                    at = 4 + 4 * side
                    gradient = edge_x_ref[at] * s1 + edge_x_ref[at + 2] * s3
                    curvature = edge_x_ref[at + 1] * s2 + edge_x_ref[at + 3] * s3
                    tend[c, z, rows] += curvature - vel[0, z, rows] * gradient
        out_copy(g).start()

    for g in range(groups):
        out_copy(g).wait()


def body(velocity, leaf_class, drag_table):
    along_x, along_y, sums_y, edge_x = constants()
    levels, n = velocity.shape[1], CELLS
    groups = levels // GROUP
    import functools

    any_space = pl.BlockSpec(memory_space=pl.ANY)
    vmem = pl.BlockSpec(memory_space=pltpu.VMEM)
    exchanged = pltpu.VMEM((2, 3, groups, 4 * GROUP, n), jnp.float32)
    return pl.pallas_call(
        functools.partial(kernel, groups),
        out_shape=jax.ShapeDtypeStruct(velocity.shape, jnp.float32),
        in_specs=[any_space, any_space, pl.BlockSpec(memory_space=pltpu.SMEM), vmem, vmem, vmem, vmem],
        out_specs=any_space,
        scratch_shapes=[
            pltpu.VMEM(velocity.shape, jnp.float32),
            pltpu.VMEM((3, levels, n, 2 * n), BF16),
            pltpu.VMEM(leaf_class.shape, jnp.int32),
            pltpu.VMEM(velocity.shape, jnp.float32),
            exchanged, exchanged, exchanged, exchanged,
            pltpu.SemaphoreType.DMA((groups,)),
            pltpu.SemaphoreType.DMA((groups,)),
            pltpu.SemaphoreType.DMA((groups,)),
            pltpu.SemaphoreType.DMA((4,)),
            pltpu.SemaphoreType.DMA((4,)),
        ],
        compiler_params=pltpu.CompilerParams(
            collective_id=0, has_side_effects=True, vmem_limit_bytes=48 * 1024 * 1024
        ),
        cost_estimate=pl.CostEstimate(flops=5_000_000_000, bytes_accessed=8_000_000, transcendentals=300_000),
    )(velocity, leaf_class, drag_table, jnp.asarray(along_x), jnp.asarray(along_y), jnp.asarray(sums_y), jnp.asarray(edge_x))


def solution(mesh):
    return jax.shard_map(
        body,
        mesh=mesh,
        in_specs=(P(None, None, "gx", "gy"), P(None, "gx", "gy"), P()),
        out_specs=P(None, None, "gx", "gy"),
        check_vma=False,
    )
```

time: 1120 us -> 23.3 us (0.02)
  the two profiles are of different devices: /device:TPU:1 before, /device:TPU:0 now
where the time goes in v1:
time: 23.3 us; the launch traced here: 23.1 us
  Pallas kernels  16.1 us (69%)
  local copies, waits for them, and re-layouts  7.02 us (30%)
    pallas_call x1, Pallas kernels, body(): pl.pallas_call(functools.partial(kernel, groups), out_shape=jax.ShapeDtyp...  16.1 us
    unnamed x13, local copies, waits for them, and re-layouts  7.02 us

profile of v1, /device:TPU:0, one launch (start us, length us, event | category | flops | bytes accessed | tf_op | source)
XLA Modules:
  0.0 23.1 jit_solution(5845826749533727985)
XLA Ops:
  0.0 0.0 copy-start
  0.0 1.2 %copy-done = s32[16,128,128]{2,1,0:T(8,128)S(1)} copy-done((s32[16,128,128]{2,1,0:T(8,128)S(1)}, s32[16,128,128]{2,1,0:T(8,128)}, u32[]{:S(2)}) %copy-start) | copy-done | bytes 1048600
  1.2 0.0 copy-start.1
  1.2 0.7 %copy-done.1 = f32[16]{0:T(128)S(1)} copy-done((f32[16]{0:T(128)S(1)}, f32[16]{0:T(128)}, u32[]{:S(2)}) %copy-start.1) | copy-done | bytes 88
  1.9 0.0 copy-start.2
  1.9 0.9 %copy-done.2 = bf16[480,256]{1,0:T(8,128)(2,1)S(1)} copy-done((bf16[480,256]{1,0:T(8,128)(2,1)S(1)}, bf16[480,256]{1,0:T(8,128)(2,1)}, u32[]{:S(2)}) %copy-start.2) | copy-done | bytes 245784
  2.8 0.0 copy-start.3
  2.8 0.9 %copy-done.3 = bf16[256,384]{1,0:T(8,128)(2,1)S(1)} copy-done((bf16[256,384]{1,0:T(8,128)(2,1)S(1)}, bf16[256,384]{1,0:T(8,128)(2,1)}, u32[]{:S(2)}) %copy-start.3) | copy-done | bytes 196632
  3.8 0.0 copy-start.4
  3.8 0.9 %copy-done.4 = f32[12,24,128]{2,1,0:T(8,128)S(1)} copy-done((f32[12,24,128]{2,1,0:T(8,128)S(1)}, f32[12,24,128]{2,1,0:T(8,128)}, u32[]{:S(2)}) %copy-start.4) | copy-done | bytes 147480
  4.7 0.0 copy-start.5
  4.7 0.7 %copy-done.5 = bf16[16,256]{1,0:T(8,128)(2,1)S(1)} copy-done((bf16[16,256]{1,0:T(8,128)(2,1)S(1)}, bf16[16,256]{1,0:T(8,128)(2,1)}, u32[]{:S(2)}) %copy-start.5) | copy-done | bytes 8216
  5.4 16.1 %shard_map.73 = f32[3,16,128,128]{3,2,1,0:T(8,128)S(1)} custom-call(f32[3,16,128,128]{3,2,1,0:T(8,128)} %vel_hbm.1, s32[16,128,128]{2,1,0:T(8,128)S(1)} %copy-done, f32[16]{0:T(128)S(1)} %copy-done.1, bf16[256,384]{1,0:T(8,128)(2,1)S(1)} %copy-done.3, bf16[480,256]{1,0:T(8,128)(2,1)S(1)} %copy-done.2, bf16[16,256]{1,0:T(8,128)(2,1)S(1)} %copy-done.5, ...), custom_call_target="tpu_custom_call" | custom-call | flops 5000000000 | bytes 8000000 | tf_op jit(solution)/shard_map/pallas_call | solution.py:263
  21.4 1.7 %copy.9 = f32[3,16,128,128]{3,2,1,0:T(8,128)} copy(f32[3,16,128,128]{3,2,1,0:T(8,128)S(1)} %shard_map.73) | data formatting | bytes 6291456
Async XLA Ops:
  0.0 1.2 %copy-start = (s32[16,128,128]{2,1,0:T(8,128)S(1)}, s32[16,128,128]{2,1,0:T(8,128)}, u32[]{:S(2)}) copy-start(s32[16,128,128]{2,1,0:T(8,128)} %leaf_hbm.1) | copy-start | bytes 3145732
  1.2 0.7 %copy-start.1 = (f32[16]{0:T(128)S(1)}, f32[16]{0:T(128)}, u32[]{:S(2)}) copy-start(f32[16]{0:T(128)} %table_ref.1) | copy-start | bytes 196
  1.9 0.9 %copy-start.2 = (bf16[480,256]{1,0:T(8,128)(2,1)S(1)}, bf16[480,256]{1,0:T(8,128)(2,1)}, u32[]{:S(2)}) copy-start(bf16[480,256]{1,0:T(8,128)(2,1)} %constant.9.clone.along_y_ref) | copy-start | bytes 737284
  2.8 0.9 %copy-start.3 = (bf16[256,384]{1,0:T(8,128)(2,1)S(1)}, bf16[256,384]{1,0:T(8,128)(2,1)}, u32[]{:S(2)}) copy-start(bf16[256,384]{1,0:T(8,128)(2,1)} %constant.8.clone.along_x_ref) | copy-start | bytes 589828
  3.8 0.9 %copy-start.4 = (f32[12,24,128]{2,1,0:T(8,128)S(1)}, f32[12,24,128]{2,1,0:T(8,128)}, u32[]{:S(2)}) copy-start(f32[12,24,128]{2,1,0:T(8,128)} %constant.11.clone.edge_x_ref) | copy-start | bytes 442372
  4.7 0.7 %copy-start.5 = (bf16[16,256]{1,0:T(8,128)(2,1)S(1)}, bf16[16,256]{1,0:T(8,128)(2,1)}, u32[]{:S(2)}) copy-start(bf16[16,256]{1,0:T(8,128)(2,1)} %constant.10.clone.sums_y_ref) | copy-start | bytes 24580

commit v2 on v1

v2 whole, which is shorter than its diff:
```python
import functools
import math

import jax
import jax.numpy as jnp
import ml_dtypes
import numpy as np
from jax import lax
from jax.experimental import pallas as pl
from jax.experimental.pallas import tpu as pltpu
from jax.sharding import PartitionSpec as P

SPACING = 2.0
CELLS = 128
GROUP = 4
EDGE = 24
BF16 = jnp.bfloat16


def kernel_of(coupling, stencil):
    root = (-1.0 + math.sqrt(1.0 - 4.0 * coupling * coupling)) / (2.0 * coupling)
    scale = 1.0 / math.sqrt(1.0 - 4.0 * coupling * coupling)

    def at(d):
        return sum(w * scale * root ** abs(d - m) for m, w in stencil.items())

    amplitude = at(2) / root**2
    return at, root, amplitude


def operators():
    h = SPACING
    a, b = 14.0 / 9.0 / (2.0 * h), 1.0 / 9.0 / (4.0 * h)
    first = {-1: a, 1: -a, -2: b, 2: -b}
    c, e = 12.0 / 11.0 / (h * h), 3.0 / 11.0 / (4.0 * h * h)
    second = {-1: c, 1: c, -2: e, 2: e, 0: -2.0 * c - 2.0 * e}
    return kernel_of(1.0 / 3.0, first), kernel_of(2.0 / 11.0, second)


def split(values):
    high = np.asarray(values, np.float64).astype(ml_dtypes.bfloat16)
    low = (np.asarray(values, np.float64) - high.astype(np.float64)).astype(ml_dtypes.bfloat16)
    return high, low


def constants():
    (k1, r1, a1), (k2, r2, a2) = operators()
    n = CELLS
    d1 = np.array([[k1(i - j) for j in range(n)] for i in range(n)])
    d2 = np.array([[k2(i - j) for j in range(n)] for i in range(n)])
    rows = np.concatenate([d1.reshape(n // 8, 8, n), d2.reshape(n // 8, 8, n)], axis=1).reshape(2 * n, n)
    high, low = split(rows)
    along_x = np.concatenate([high, high, low], axis=1)
    high, low = split(np.concatenate([d1.T, d2.T], axis=1))
    i = np.arange(n)
    e1, e2 = k1(1) - a1 * r1, k2(1) - a2 * r2
    zero = np.zeros(n)
    first, last = (i == 0) * 1.0, (i == n - 1) * 1.0
    before = np.stack([
        np.concatenate([r1**i, zero]),
        np.concatenate([zero, r2**i]),
        np.concatenate([e1 * first, e2 * first]),
    ])
    after = np.stack([
        np.concatenate([-(r1 ** (n - 1 - i)), zero]),
        np.concatenate([zero, r2 ** (n - 1 - i)]),
        np.concatenate([-e1 * last, e2 * last]),
    ])
    spread = np.repeat(np.concatenate([before, after]), GROUP, axis=0)
    spread_high, spread_low = split(spread)
    blank = np.zeros((8, 2 * n), spread_high.dtype)
    along_y = np.concatenate([high, high, low, spread_high, spread_high, spread_low, blank], axis=0)
    forward = np.stack([a1 * r1 ** (n - i.astype(float)), a2 * r2 ** (n - i.astype(float)), last, zero])
    backward = np.stack([a1 * r1 ** (1.0 + i), a2 * r2 ** (1.0 + i), first, zero])
    high, low = split(np.concatenate([forward, backward]))
    sums_y = np.concatenate(
        [np.concatenate([high, high], axis=1), np.concatenate([low, np.zeros_like(low)], axis=1)], axis=0
    )
    lanes = np.ones((1, n))
    edge_x = np.stack([
        forward[0, n - EDGE :, None] * lanes,
        forward[1, n - EDGE :, None] * lanes,
        backward[0, :EDGE, None] * lanes,
        backward[1, :EDGE, None] * lanes,
        (r1 ** i[:EDGE])[:, None] * lanes,
        (r2 ** i[:EDGE])[:, None] * lanes,
        (e1 * first)[:EDGE, None] * lanes,
        (e2 * first)[:EDGE, None] * lanes,
        (-(r1 ** (n - 1 - i)))[n - EDGE :, None] * lanes,
        (r2 ** (n - 1 - i))[n - EDGE :, None] * lanes,
        (-e1 * last)[n - EDGE :, None] * lanes,
        (e2 * last)[n - EDGE :, None] * lanes,
    ]).astype(np.float32)
    return along_x, along_y, sums_y, edge_x


def dot(a, b):
    return lax.dot_general(a, b, (((1,), (0,)), ((), ())), preferred_element_type=jnp.float32)


def dot_transposed(a, b):
    return lax.dot_general(a, b, (((1,), (1,)), ((), ())), preferred_element_type=jnp.float32)


def solve_y(g, vel, parts, tend, recv_y, along_y, store):
    n = CELLS
    values = 3 * GROUP
    lane = lax.broadcasted_iota(jnp.int32, (n, 80), 1)
    spread = []
    for c in range(3):
        got = jnp.concatenate([recv_y[side, g, c * values : (c + 1) * values] for side in range(2)], axis=0)
        high = got.astype(BF16).astype(jnp.float32)
        low = (got - high).astype(BF16).astype(jnp.float32)
        blank = jnp.zeros((8, n), jnp.float32)
        spread.append(jnp.concatenate([high, low, high, blank], axis=0).T.astype(BF16))
    for k in range(GROUP):
        z = g * GROUP + k
        mask = (lane % GROUP) == k
        left = []
        for c in range(3):
            mine = jnp.where(mask, spread[c], jnp.zeros_like(spread[c]))
            left.append(jnp.concatenate([parts[c, z], parts[c, z, :, :n], mine], axis=1))
        both = dot(jnp.concatenate(left, axis=0), along_y[...])
        for c in range(3):
            gradient = both[c * n : (c + 1) * n, :n]
            curvature = both[c * n : (c + 1) * n, n:]
            store(c, k, tend[c, z] + curvature - vel[1, z] * gradient)


def first_kernel(
    groups, solved, vel_hbm, leaf_hbm, table_hbm, along_x_hbm, along_y_hbm, sums_y_hbm, edge_x_hbm,
    vel, parts, tend, recv_x, recv_y,
    leaf, send_x, send_y, along_x, along_y, sums_y, edge_x, table_ref,
    vel_sem, leaf_sem, const_sem, send_sem, recv_sem, send_y_sem, recv_y_sem,
):
    n = CELLS
    half = 2 * GROUP
    halves = groups // 2

    consts = [
        pltpu.make_async_copy(a, b, const_sem.at[i])
        for i, (a, b) in enumerate(
            [(edge_x_hbm, edge_x), (sums_y_hbm, sums_y), (along_x_hbm, along_x), (along_y_hbm, along_y),
             (table_hbm, table_ref)]
        )
    ]

    def levels(g):
        return pl.ds(g * GROUP, GROUP)

    def edge_copy(h, side):
        at = (slice(None), pl.ds(h * half, half), pl.ds(side * (n - EDGE), EDGE))
        return pltpu.make_async_copy(vel_hbm.at[at], vel.at[at], vel_sem.at[side, h])

    def middle_copy(g):
        at = (slice(None), levels(g), pl.ds(EDGE, n - 2 * EDGE))
        return pltpu.make_async_copy(vel_hbm.at[at], vel.at[at], vel_sem.at[2, g])

    def leaf_copy(g):
        return pltpu.make_async_copy(leaf_hbm.at[levels(g)], leaf.at[levels(g)], leaf_sem.at[g])

    consts[0].start()
    for h in range(halves):
        for side in range(2):
            edge_copy(h, side).start()
    consts[1].start()
    for g in range(groups):
        middle_copy(g).start()
    consts[4].start()
    consts[2].start()
    for g in range(groups):
        leaf_copy(g).start()
    consts[3].start()

    mx, my = lax.axis_index("gx"), lax.axis_index("gy")
    nx, ny = lax.axis_size("gx"), lax.axis_size("gy")
    targets = [
        {"gx": lax.rem(mx + 1, nx)},
        {"gx": lax.rem(mx + nx - 1, nx)},
        {"gy": lax.rem(my + 1, ny)},
        {"gy": lax.rem(my + ny - 1, ny)},
    ]
    barrier = pltpu.get_barrier_semaphore()
    for target in targets:
        pl.semaphore_signal(barrier, inc=1, device_id=target, device_id_type=pl.DeviceIdType.MESH)

    def send_x_copy(side):
        return pltpu.make_async_remote_copy(
            src_ref=send_x.at[side], dst_ref=recv_x.at[side],
            send_sem=send_sem.at[side], recv_sem=recv_sem.at[side],
            device_id=targets[side], device_id_type=pl.DeviceIdType.MESH,
        )

    def send_y_copy(side, g):
        return pltpu.make_async_remote_copy(
            src_ref=send_y.at[side, g], dst_ref=recv_y.at[side, g],
            send_sem=send_y_sem.at[side, g], recv_sem=recv_y_sem.at[side, g],
            device_id=targets[2 + side], device_id_type=pl.DeviceIdType.MESH,
        )

    consts[0].wait()

    @pl.loop(0, halves)
    def _(h):
        edge_copy(h, 0).wait()
        edge_copy(h, 1).wait()
        for c in range(3):
            for k in range(half):
                top, bottom = vel[c, h * half + k, :EDGE], vel[c, h * half + k, n - EDGE :]
                for q in range(2):
                    row = (c * 3 + q) * half + k
                    send_x[0, h, row : row + 1] = jnp.sum(edge_x[q] * bottom, axis=0, keepdims=True)
                    send_x[1, h, row : row + 1] = jnp.sum(edge_x[2 + q] * top, axis=0, keepdims=True)
                row = (c * 3 + 2) * half + k
                send_x[0, h, row : row + 1] = bottom[EDGE - 1 :]
                send_x[1, h, row : row + 1] = top[:1]

    pl.semaphore_wait(barrier, 4)
    for side in range(2):
        send_x_copy(side).start()

    consts[1].wait()

    @pl.loop(0, groups)
    def _(g):
        middle_copy(g).wait()
        for c in range(3):
            for k in range(GROUP):
                values = vel[c, g * GROUP + k]
                high = values.astype(BF16)
                parts[c, g * GROUP + k, :, :n] = high
                parts[c, g * GROUP + k, :, n:] = (values - high.astype(jnp.float32)).astype(BF16)
            for k in range(0, GROUP, 2):
                pair = parts[c, pl.ds(g * GROUP + k, 2)].reshape(2 * n, 2 * n)
                sums = dot_transposed(sums_y[...], pair)
                sums = sums[:8] + sums[8:]
                for j in range(2):
                    for q in range(3):
                        row = (c * 3 + q) * GROUP + k + j
                        send_y[0, g, row : row + 1] = sums[q : q + 1, j * n : (j + 1) * n]
                        send_y[1, g, row : row + 1] = sums[4 + q : 5 + q, j * n : (j + 1) * n]
        for side in range(2):
            send_y[side, g, 9 * GROUP :] = jnp.zeros((4, n), jnp.float32)
            send_y_copy(side, g).start()

    lane = lax.broadcasted_iota(jnp.int32, (n, n), 1)
    consts[4].wait()
    table = jnp.zeros((n, n), jnp.float32)
    for k in range(table_ref.shape[0]):
        table = jnp.where(lane == k, table_ref[k], table)
    consts[2].wait()

    @pl.loop(0, groups)
    def _(g):
        leaf_copy(g).wait()
        for k in range(0, GROUP, 2):
            z = (g * GROUP + k, g * GROUP + k + 1)
            drag = []
            for j in range(2):
                speed = jnp.sqrt(vel[0, z[j]] ** 2 + vel[1, z[j]] ** 2 + vel[2, z[j]] ** 2)
                drag.append(jnp.take_along_axis(table, leaf[z[j]], axis=1) * speed)
            for c in range(3):
                high = jnp.concatenate([parts[c, z[0], :, :n], parts[c, z[1], :, :n]], axis=1)
                low = jnp.concatenate([parts[c, z[0], :, n:], parts[c, z[1], :, n:]], axis=1)
                both = dot(along_x[...], jnp.concatenate([high, low, high], axis=0))
                both = both.reshape(n // 8, 2, 8, 2 * n)
                for j in range(2):
                    gradient = both[:, 0, :, j * n : (j + 1) * n].reshape(n, n)
                    curvature = both[:, 1, :, j * n : (j + 1) * n].reshape(n, n)
                    tend[c, z[j]] = curvature - vel[0, z[j]] * gradient - drag[j] * vel[c, z[j]]

    consts[3].wait()

    @pl.loop(0, groups)
    def _(g):
        for side in range(2):
            send_y_copy(side, g).wait()

        @pl.when(g < solved)
        def _():
            def store(c, k, values):
                tend[c, g * GROUP + k] = values

            solve_y(g, vel, parts, tend, recv_y, along_y, store)

    for side in range(2):
        send_x_copy(side).wait()


def second_kernel(
    groups, solved, vel, parts, tend, recv_x, recv_y, along_y_hbm, edge_x_hbm, out_hbm,
    edges, rest, along_y, edge_x, const_sem, middle_sem, edge_sem, rest_sem,
):
    n = CELLS
    half = 2 * GROUP
    consts = [
        pltpu.make_async_copy(a, b, const_sem.at[i])
        for i, (a, b) in enumerate([(edge_x_hbm, edge_x), (along_y_hbm, along_y)])
    ]
    for copy in consts:
        copy.start()

    def middle_copy(g):
        at = (slice(None), pl.ds(g * GROUP, GROUP), pl.ds(EDGE, n - 2 * EDGE))
        return pltpu.make_async_copy(tend.at[at], out_hbm.at[at], middle_sem.at[g])

    def edge_copy(g, side):
        at = (slice(None), pl.ds(g * GROUP, GROUP), pl.ds(side * (n - EDGE), EDGE))
        source = edges.at[side, :, pl.ds(g * GROUP, GROUP)]
        return pltpu.make_async_copy(source, out_hbm.at[at], edge_sem.at[side, g])

    def rest_copy(z):
        return pltpu.make_async_copy(rest.at[:, z - solved * GROUP], out_hbm.at[:, z], rest_sem.at[z - solved * GROUP])

    def added(c, g, k, side):
        h, lev = g // 2, (g % 2) * GROUP + k
        s1, s2, s3 = (recv_x[side, h, (c * 3 + q) * half + lev : (c * 3 + q) * half + lev + 1] for q in range(3))
        gradient = edge_x[4 + 4 * side] * s1 + edge_x[6 + 4 * side] * s3
        curvature = edge_x[5 + 4 * side] * s2 + edge_x[7 + 4 * side] * s3
        return curvature - vel[0, g * GROUP + k, side * (n - EDGE) : side * (n - EDGE) + EDGE] * gradient

    for g in range(solved):
        middle_copy(g).start()
    consts[0].wait()
    for g in range(solved):
        for side in range(2):
            rows = slice(side * (n - EDGE), side * (n - EDGE) + EDGE)
            for c in range(3):
                for k in range(GROUP):
                    edges[side, c, g * GROUP + k] = tend[c, g * GROUP + k, rows] + added(c, g, k, side)
            edge_copy(g, side).start()
    consts[1].wait()
    for g in range(solved, groups):
        base = (g - solved) * GROUP

        def store(c, k, values):
            rest[c, base + k] = values
            for side in range(2):
                rows = slice(side * (n - EDGE), side * (n - EDGE) + EDGE)
                rest[c, base + k, rows] += added(c, g, k, side)
            if c == 2:
                rest_copy(g * GROUP + k).start()

        solve_y(g, vel, parts, tend, recv_y, along_y, store)
    for g in range(solved):
        middle_copy(g).wait()
        for side in range(2):
            edge_copy(g, side).wait()
    for z in range(solved * GROUP, groups * GROUP):
        rest_copy(z).wait()


def in_hbm(array):
    return pltpu.with_memory_space_constraint(array, pltpu.HBM)


def body(velocity, leaf_class, drag_table):
    along_x, along_y, sums_y, edge_x = (in_hbm(jnp.asarray(a)) for a in constants())
    velocity, leaf_class, drag_table = in_hbm(velocity), in_hbm(leaf_class), in_hbm(drag_table)
    levels, n = velocity.shape[1], CELLS
    groups = levels // GROUP
    solved = groups - 1
    hbm = pl.BlockSpec(memory_space=pltpu.HBM)
    vmem = pl.BlockSpec(memory_space=pltpu.VMEM)
    dma = pltpu.SemaphoreType.DMA
    sums_along_x = (2, groups // 2, 18 * GROUP, n)
    sums_along_y = (2, groups, 10 * GROUP, n)
    held = [
        jax.ShapeDtypeStruct(velocity.shape, jnp.float32),
        jax.ShapeDtypeStruct((3, levels, n, 2 * n), BF16),
        jax.ShapeDtypeStruct(velocity.shape, jnp.float32),
        jax.ShapeDtypeStruct(sums_along_x, jnp.float32),
        jax.ShapeDtypeStruct(sums_along_y, jnp.float32),
    ]
    held = pl.pallas_call(
        functools.partial(first_kernel, groups, solved),
        out_shape=held,
        in_specs=[hbm, hbm, hbm, hbm, hbm, hbm, hbm],
        out_specs=[vmem] * 5,
        scratch_shapes=[
            pltpu.VMEM(leaf_class.shape, jnp.int32),
            pltpu.VMEM(sums_along_x, jnp.float32),
            pltpu.VMEM(sums_along_y, jnp.float32),
            pltpu.VMEM(along_x.shape, BF16),
            pltpu.VMEM(along_y.shape, BF16),
            pltpu.VMEM(sums_y.shape, BF16),
            pltpu.VMEM(edge_x.shape, jnp.float32),
            pltpu.SMEM(drag_table.shape, jnp.float32),
            dma((3, groups)), dma((groups,)), dma((5,)), dma((2,)), dma((2,)), dma((2, groups)), dma((2, groups)),
        ],
        compiler_params=pltpu.CompilerParams(
            collective_id=0, has_side_effects=True, vmem_limit_bytes=40 * 1024 * 1024
        ),
        cost_estimate=pl.CostEstimate(flops=4_000_000_000, bytes_accessed=5_000_000, transcendentals=300_000),
        name="exchange_and_solve",
    )(velocity, leaf_class, drag_table, along_x, along_y, sums_y, edge_x)
    return pl.pallas_call(
        functools.partial(second_kernel, groups, solved),
        out_shape=jax.ShapeDtypeStruct(velocity.shape, jnp.float32),
        in_specs=[vmem] * 5 + [hbm, hbm],
        out_specs=hbm,
        scratch_shapes=[
            pltpu.VMEM((2, 3, levels, EDGE, n), jnp.float32),
            pltpu.VMEM((3, (groups - solved) * GROUP, n, n), jnp.float32),
            pltpu.VMEM(along_y.shape, BF16),
            pltpu.VMEM(edge_x.shape, jnp.float32),
            dma((2,)), dma((groups,)), dma((2, groups)), dma(((groups - solved) * GROUP,)),
        ],
        compiler_params=pltpu.CompilerParams(vmem_limit_bytes=40 * 1024 * 1024),
        cost_estimate=pl.CostEstimate(flops=1_000_000_000, bytes_accessed=3_000_000, transcendentals=0),
        name="finish",
    )(*held, along_y, edge_x)


def solution(mesh):
    return jax.shard_map(
        body,
        mesh=mesh,
        in_specs=(P(None, None, "gx", "gy"), P(None, "gx", "gy"), P()),
        out_specs=P(None, None, "gx", "gy"),
        check_vma=False,
    )
```

time: 23.3 us -> 16.1 us (0.69)
  the two profiles are of different devices: /device:TPU:0 before, /device:TPU:16 now
where the time goes in v2:
time: 16.1 us; the launch traced here: 16 us
  Pallas kernels  16 us (99%)
    pallas_call x1, Pallas kernels, body(): pl.pallas_call(functools.partial(first_kernel, groups, solved), out_shape...  13.1 us
    pallas_call x1, Pallas kernels, body(): pl.pallas_call(functools.partial(second_kernel, groups, solved), out_shap...  2.92 us

profile of v2, /device:TPU:16, one launch (start us, length us, event | category | flops | bytes accessed | tf_op | source)
XLA Modules:
  0.0 16.0 jit_solution(8535791109605726330)
XLA Ops:
  0.0 13.1 %exchange_and_solve.1 = (f32[3,16,128,128]{3,2,1,0:T(8,128)S(1)}, bf16[3,16,128,256]{3,2,1,0:T(8,128)(2,1)S(1)}, f32[3,16,128,128]{3,2,1,0:T(8,128)S(1)}, f32[2,...) custom-call(f32[3,16,128,128]{3,2,1,0:T(8,128)} %vel_hbm.1, s32[16,128,128]{2,1,0:T(8,128)} %leaf_hbm.1, f32[16]{0:T(128)} %table_hbm.1, ...), custom_call_target="tpu_custom_call" | custom-call | flops 4000000000 | bytes 5000000 | tf_op jit(solution)/shard_map/exchange_and_solve/pallas_call | solution.py:375
  13.1 2.9 %finish.1 = f32[3,16,128,128]{3,2,1,0:T(8,128)} custom-call(f32[3,16,128,128]{3,2,1,0:T(8,128)S(1)} %get-tuple-element.10.vel, bf16[3,16,128,256]{3,2,1,0:T(8,128)(2,1)S(1)} %get-tuple-element.11.parts, f32[3,16,128,128]{3,2,1,0:T(8,128)S(1)} %get-tuple-element.12.tend, f32[2,2,72,128]{3,2,1,0:T(8,128)S(1)} %get-tuple-element.13.recv_x, ...), custom_call_target="tpu_custom_call" | custom-call | flops 1000000000 | bytes 3000000 | tf_op jit(solution)/shard_map/finish/pallas_call | solution.py:397

commit v3 on v2

--- a/solution.py
+++ b/solution.py
@@ -69,7 +69,8 @@
     spread = np.repeat(np.concatenate([before, after]), GROUP, axis=0)
     spread_high, spread_low = split(spread)
     blank = np.zeros((8, 2 * n), spread_high.dtype)
-    along_y = np.concatenate([high, high, low, spread_high, spread_high, spread_low, blank], axis=0)
+    along_y = np.concatenate([high, high, low], axis=0)
+    spread_y = np.concatenate([spread_high, spread_high, spread_low, blank], axis=0)
     forward = np.stack([a1 * r1 ** (n - i.astype(float)), a2 * r2 ** (n - i.astype(float)), last, zero])
     backward = np.stack([a1 * r1 ** (1.0 + i), a2 * r2 ** (1.0 + i), first, zero])
     high, low = split(np.concatenate([forward, backward]))
@@ -91,7 +92,7 @@
         (-e1 * last)[n - EDGE :, None] * lanes,
         (e2 * last)[n - EDGE :, None] * lanes,
     ]).astype(np.float32)
-    return along_x, along_y, sums_y, edge_x
+    return along_x, along_y, spread_y, sums_y, edge_x
 
 
 def dot(a, b):
@@ -102,35 +103,10 @@
     return lax.dot_general(a, b, (((1,), (1,)), ((), ())), preferred_element_type=jnp.float32)
 
 
-def solve_y(g, vel, parts, tend, recv_y, along_y, store):
-    n = CELLS
-    values = 3 * GROUP
-    lane = lax.broadcasted_iota(jnp.int32, (n, 80), 1)
-    spread = []
-    for c in range(3):
-        got = jnp.concatenate([recv_y[side, g, c * values : (c + 1) * values] for side in range(2)], axis=0)
-        high = got.astype(BF16).astype(jnp.float32)
-        low = (got - high).astype(BF16).astype(jnp.float32)
-        blank = jnp.zeros((8, n), jnp.float32)
-        spread.append(jnp.concatenate([high, low, high, blank], axis=0).T.astype(BF16))
-    for k in range(GROUP):
-        z = g * GROUP + k
-        mask = (lane % GROUP) == k
-        left = []
-        for c in range(3):
-            mine = jnp.where(mask, spread[c], jnp.zeros_like(spread[c]))
-            left.append(jnp.concatenate([parts[c, z], parts[c, z, :, :n], mine], axis=1))
-        both = dot(jnp.concatenate(left, axis=0), along_y[...])
-        for c in range(3):
-            gradient = both[c * n : (c + 1) * n, :n]
-            curvature = both[c * n : (c + 1) * n, n:]
-            store(c, k, tend[c, z] + curvature - vel[1, z] * gradient)
-
-
 def first_kernel(
-    groups, solved, vel_hbm, leaf_hbm, table_hbm, along_x_hbm, along_y_hbm, sums_y_hbm, edge_x_hbm,
-    vel, parts, tend, recv_x, recv_y,
-    leaf, send_x, send_y, along_x, along_y, sums_y, edge_x, table_ref,
+    groups, vel_hbm, leaf_hbm, table_hbm, along_x_hbm, along_y_hbm, spread_y_hbm, sums_y_hbm, edge_x_hbm,
+    vel, tend, recv_x, recv_y, spread_y, edge_x,
+    parts, leaf, send_x, send_y, along_x, along_y, sums_y, table_ref,
     vel_sem, leaf_sem, const_sem, send_sem, recv_sem, send_y_sem, recv_y_sem,
 ):
     n = CELLS
@@ -141,7 +117,7 @@
         pltpu.make_async_copy(a, b, const_sem.at[i])
         for i, (a, b) in enumerate(
             [(edge_x_hbm, edge_x), (sums_y_hbm, sums_y), (along_x_hbm, along_x), (along_y_hbm, along_y),
-             (table_hbm, table_ref)]
+             (table_hbm, table_ref), (spread_y_hbm, spread_y)]
         )
     ]
 
@@ -171,6 +147,7 @@
     for g in range(groups):
         leaf_copy(g).start()
     consts[3].start()
+    consts[5].start()
 
     mx, my = lax.axis_index("gx"), lax.axis_index("gy")
     nx, ny = lax.axis_size("gx"), lax.axis_size("gy")
@@ -273,81 +250,63 @@
 
     @pl.loop(0, groups)
     def _(g):
+        for k in range(GROUP):
+            z = g * GROUP + k
+            left = [jnp.concatenate([parts[c, z], parts[c, z, :, :n]], axis=1) for c in range(3)]
+            both = dot(jnp.concatenate(left, axis=0), along_y[...])
+            for c in range(3):
+                gradient = both[c * n : (c + 1) * n, :n]
+                curvature = both[c * n : (c + 1) * n, n:]
+                tend[c, z] += curvature - vel[1, z] * gradient
+
+    @pl.loop(0, groups)
+    def _(g):
         for side in range(2):
             send_y_copy(side, g).wait()
 
-        @pl.when(g < solved)
-        def _():
-            def store(c, k, values):
-                tend[c, g * GROUP + k] = values
-
-            solve_y(g, vel, parts, tend, recv_y, along_y, store)
-
     for side in range(2):
         send_x_copy(side).wait()
-
-
-def second_kernel(
-    groups, solved, vel, parts, tend, recv_x, recv_y, along_y_hbm, edge_x_hbm, out_hbm,
-    edges, rest, along_y, edge_x, const_sem, middle_sem, edge_sem, rest_sem,
-):
+    consts[5].wait()
+
+
+def second_kernel(groups, vel, tend, recv_x, recv_y, spread_y, edge_x, out_hbm, result, out_sem):
     n = CELLS
     half = 2 * GROUP
-    consts = [
-        pltpu.make_async_copy(a, b, const_sem.at[i])
-        for i, (a, b) in enumerate([(edge_x_hbm, edge_x), (along_y_hbm, along_y)])
-    ]
-    for copy in consts:
-        copy.start()
-
-    def middle_copy(g):
-        at = (slice(None), pl.ds(g * GROUP, GROUP), pl.ds(EDGE, n - 2 * EDGE))
-        return pltpu.make_async_copy(tend.at[at], out_hbm.at[at], middle_sem.at[g])
-
-    def edge_copy(g, side):
-        at = (slice(None), pl.ds(g * GROUP, GROUP), pl.ds(side * (n - EDGE), EDGE))
-        source = edges.at[side, :, pl.ds(g * GROUP, GROUP)]
-        return pltpu.make_async_copy(source, out_hbm.at[at], edge_sem.at[side, g])
-
-    def rest_copy(z):
-        return pltpu.make_async_copy(rest.at[:, z - solved * GROUP], out_hbm.at[:, z], rest_sem.at[z - solved * GROUP])
-
-    def added(c, g, k, side):
-        h, lev = g // 2, (g % 2) * GROUP + k
-        s1, s2, s3 = (recv_x[side, h, (c * 3 + q) * half + lev : (c * 3 + q) * half + lev + 1] for q in range(3))
-        gradient = edge_x[4 + 4 * side] * s1 + edge_x[6 + 4 * side] * s3
-        curvature = edge_x[5 + 4 * side] * s2 + edge_x[7 + 4 * side] * s3
-        return curvature - vel[0, g * GROUP + k, side * (n - EDGE) : side * (n - EDGE) + EDGE] * gradient
-
-    for g in range(solved):
-        middle_copy(g).start()
-    consts[0].wait()
-    for g in range(solved):
-        for side in range(2):
-            rows = slice(side * (n - EDGE), side * (n - EDGE) + EDGE)
+    values = 3 * GROUP
+
+    def out_copy(z):
+        return pltpu.make_async_copy(result.at[:, z], out_hbm.at[:, z], out_sem.at[z])
+
+    lane = lax.broadcasted_iota(jnp.int32, (n, 80), 1)
+    for g in range(groups):
+        spread = []
+        for c in range(3):
+            got = jnp.concatenate([recv_y[side, g, c * values : (c + 1) * values] for side in range(2)], axis=0)
+            high = got.astype(BF16).astype(jnp.float32)
+            low = (got - high).astype(BF16).astype(jnp.float32)
+            blank = jnp.zeros((8, n), jnp.float32)
+            spread.append(jnp.concatenate([high, low, high, blank], axis=0).T.astype(BF16))
+        for k in range(GROUP):
+            z = g * GROUP + k
+            mask = (lane % GROUP) == k
+            left = [jnp.where(mask, s, jnp.zeros_like(s)) for s in spread]
+            both = dot(jnp.concatenate(left, axis=0), spread_y[...])
             for c in range(3):
-                for k in range(GROUP):
-                    edges[side, c, g * GROUP + k] = tend[c, g * GROUP + k, rows] + added(c, g, k, side)
-            edge_copy(g, side).start()
-    consts[1].wait()
-    for g in range(solved, groups):
-        base = (g - solved) * GROUP
-
-        def store(c, k, values):
-            rest[c, base + k] = values
-            for side in range(2):
-                rows = slice(side * (n - EDGE), side * (n - EDGE) + EDGE)
-                rest[c, base + k, rows] += added(c, g, k, side)
-            if c == 2:
-                rest_copy(g * GROUP + k).start()
-
-        solve_y(g, vel, parts, tend, recv_y, along_y, store)
-    for g in range(solved):
-        middle_copy(g).wait()
-        for side in range(2):
-            edge_copy(g, side).wait()
-    for z in range(solved * GROUP, groups * GROUP):
-        rest_copy(z).wait()
+                gradient = both[c * n : (c + 1) * n, :n]
+                curvature = both[c * n : (c + 1) * n, n:]
+                values_z = tend[c, z] + curvature - vel[1, z] * gradient
+                ends = []
+                for side in range(2):
+                    h, at = g // 2, c * 3 * half + (g % 2) * GROUP + k
+                    s1, s2, s3 = (recv_x[side, h, at + q * half : at + q * half + 1] for q in range(3))
+                    gradient = edge_x[4 + 4 * side] * s1 + edge_x[6 + 4 * side] * s3
+                    curvature = edge_x[5 + 4 * side] * s2 + edge_x[7 + 4 * side] * s3
+                    rows = slice(side * (n - EDGE), side * (n - EDGE) + EDGE)
+                    ends.append(values_z[rows] + curvature - vel[0, z, rows] * gradient)
+                result[c, z] = jnp.concatenate([ends[0], values_z[EDGE : n - EDGE], ends[1]], axis=0)
+            out_copy(z).start()
+    for z in range(groups * GROUP):
+        out_copy(z).wait()
 
 
 def in_hbm(array):
@@ -355,11 +314,10 @@
 
 
 def body(velocity, leaf_class, drag_table):
-    along_x, along_y, sums_y, edge_x = (in_hbm(jnp.asarray(a)) for a in constants())
+    along_x, along_y, spread_y, sums_y, edge_x = (in_hbm(jnp.asarray(a)) for a in constants())
     velocity, leaf_class, drag_table = in_hbm(velocity), in_hbm(leaf_class), in_hbm(drag_table)
     levels, n = velocity.shape[1], CELLS
     groups = levels // GROUP
-    solved = groups - 1
     hbm = pl.BlockSpec(memory_space=pltpu.HBM)
     vmem = pl.BlockSpec(memory_space=pltpu.VMEM)
     dma = pltpu.SemaphoreType.DMA
@@ -367,49 +325,44 @@
     sums_along_y = (2, groups, 10 * GROUP, n)
     held = [
         jax.ShapeDtypeStruct(velocity.shape, jnp.float32),
-        jax.ShapeDtypeStruct((3, levels, n, 2 * n), BF16),
         jax.ShapeDtypeStruct(velocity.shape, jnp.float32),
         jax.ShapeDtypeStruct(sums_along_x, jnp.float32),
         jax.ShapeDtypeStruct(sums_along_y, jnp.float32),
+        jax.ShapeDtypeStruct(spread_y.shape, BF16),
+        jax.ShapeDtypeStruct(edge_x.shape, jnp.float32),
     ]
     held = pl.pallas_call(
-        functools.partial(first_kernel, groups, solved),
+        functools.partial(first_kernel, groups),
         out_shape=held,
-        in_specs=[hbm, hbm, hbm, hbm, hbm, hbm, hbm],
-        out_specs=[vmem] * 5,
+        in_specs=[hbm] * 8,
+        out_specs=[vmem] * 6,
         scratch_shapes=[
+            pltpu.VMEM((3, levels, n, 2 * n), BF16),
             pltpu.VMEM(leaf_class.shape, jnp.int32),
             pltpu.VMEM(sums_along_x, jnp.float32),
             pltpu.VMEM(sums_along_y, jnp.float32),
             pltpu.VMEM(along_x.shape, BF16),
             pltpu.VMEM(along_y.shape, BF16),
             pltpu.VMEM(sums_y.shape, BF16),
-            pltpu.VMEM(edge_x.shape, jnp.float32),
             pltpu.SMEM(drag_table.shape, jnp.float32),
-            dma((3, groups)), dma((groups,)), dma((5,)), dma((2,)), dma((2,)), dma((2, groups)), dma((2, groups)),
+            dma((3, groups)), dma((groups,)), dma((6,)), dma((2,)), dma((2,)), dma((2, groups)), dma((2, groups)),
         ],
         compiler_params=pltpu.CompilerParams(
             collective_id=0, has_side_effects=True, vmem_limit_bytes=40 * 1024 * 1024
         ),
         cost_estimate=pl.CostEstimate(flops=4_000_000_000, bytes_accessed=5_000_000, transcendentals=300_000),
         name="exchange_and_solve",
-    )(velocity, leaf_class, drag_table, along_x, along_y, sums_y, edge_x)
+    )(velocity, leaf_class, drag_table, along_x, along_y, spread_y, sums_y, edge_x)
     return pl.pallas_call(
-        functools.partial(second_kernel, groups, solved),
+        functools.partial(second_kernel, groups),
         out_shape=jax.ShapeDtypeStruct(velocity.shape, jnp.float32),
-        in_specs=[vmem] * 5 + [hbm, hbm],
+        in_specs=[vmem] * 6,
         out_specs=hbm,
-        scratch_shapes=[
-            pltpu.VMEM((2, 3, levels, EDGE, n), jnp.float32),
-            pltpu.VMEM((3, (groups - solved) * GROUP, n, n), jnp.float32),
-            pltpu.VMEM(along_y.shape, BF16),
-            pltpu.VMEM(edge_x.shape, jnp.float32),
-            dma((2,)), dma((groups,)), dma((2, groups)), dma(((groups - solved) * GROUP,)),
-        ],
+        scratch_shapes=[pltpu.VMEM(velocity.shape, jnp.float32), dma((levels,))],
         compiler_params=pltpu.CompilerParams(vmem_limit_bytes=40 * 1024 * 1024),
         cost_estimate=pl.CostEstimate(flops=1_000_000_000, bytes_accessed=3_000_000, transcendentals=0),
         name="finish",
-    )(*held, along_y, edge_x)
+    )(*held)
 
 
 def solution(mesh):

time: 16.1 us -> 15.2 us (0.944)
  the two profiles are of different devices: /device:TPU:16 before, /device:TPU:6 now
where the time goes in v3:
time: 15.2 us; the launch traced here: 15.1 us
  Pallas kernels  15.1 us (99%)
    pallas_call x1, Pallas kernels, body(): pl.pallas_call(functools.partial(first_kernel, groups), out_shape=held, i...  12.8 us
    pallas_call x1, Pallas kernels, body(): pl.pallas_call(functools.partial(second_kernel, groups), out_shape=jax.Sh...  2.27 us

profile of v3, /device:TPU:6, one launch (start us, length us, event | category | flops | bytes accessed | tf_op | source)
XLA Modules:
  0.0 15.1 jit_solution(17457253508838366858)
XLA Ops:
  0.0 12.8 %exchange_and_solve.1 = (f32[3,16,128,128]{3,2,1,0:T(8,128)S(1)}, f32[3,16,128,128]{3,2,1,0:T(8,128)S(1)}, f32[2,2,72,128]{3,2,1,0:T(8,128)S(1)}, f32[2,4,40,128...) custom-call(f32[3,16,128,128]{3,2,1,0:T(8,128)} %vel_hbm.1, s32[16,128,128]{2,1,0:T(8,128)} %leaf_hbm.1, ...), custom_call_target="tpu_custom_call" | custom-call | flops 4000000000 | bytes 5000000 | tf_op jit(solution)/shard_map/exchange_and_solve/pallas_call | solution.py:334
  12.8 2.3 %finish.1 = f32[3,16,128,128]{3,2,1,0:T(8,128)} custom-call(f32[3,16,128,128]{3,2,1,0:T(8,128)S(1)} %get-tuple-element.11.vel, f32[3,16,128,128]{3,2,1,0:T(8,128)S(1)} %get-tuple-element.12.tend, f32[2,2,72,128]{3,2,1,0:T(8,128)S(1)} %get-tuple-element.13.recv_x, f32[2,4,40,128]{3,2,1,0:T(8,128)S(1)} %get-tuple-element.14.recv_y, ...), custom_call_target="tpu_custom_call" | custom-call | flops 1000000000 | bytes 3000000 | tf_op jit(solution)/shard_map/finish/pallas_call | solution.py:356

commit v4 on v3

--- a/solution.py
+++ b/solution.py
@@ -107,7 +107,7 @@
     groups, vel_hbm, leaf_hbm, table_hbm, along_x_hbm, along_y_hbm, spread_y_hbm, sums_y_hbm, edge_x_hbm,
     vel, tend, recv_x, recv_y, spread_y, edge_x,
     parts, leaf, send_x, send_y, along_x, along_y, sums_y, table_ref,
-    vel_sem, leaf_sem, const_sem, send_sem, recv_sem, send_y_sem, recv_y_sem,
+    vel_sem, leaf_sem, const_sem, send_sem, recv_sem,
 ):
     n = CELLS
     half = 2 * GROUP
@@ -157,23 +157,42 @@
         {"gy": lax.rem(my + 1, ny)},
         {"gy": lax.rem(my + ny - 1, ny)},
     ]
+    first, last = my == 0, my == ny - 1
     barrier = pltpu.get_barrier_semaphore()
-    for target in targets:
+    for target in (targets[0], targets[1], targets[3]):
         pl.semaphore_signal(barrier, inc=1, device_id=target, device_id_type=pl.DeviceIdType.MESH)
 
-    def send_x_copy(side):
+    @pl.when(jnp.logical_not(last))
+    def _():
+        pl.semaphore_signal(barrier, inc=1, device_id=targets[2], device_id_type=pl.DeviceIdType.MESH)
+
+    late = jnp.logical_or(mx == nx - 1, last)
+    sending_step = jnp.where(late, 0, jnp.where(mx == 0, groups, groups // 2))
+    sending_step = jnp.where(jnp.logical_and(last, mx == 0), groups // 2, sending_step)
+
+    def sum_copy(t):
+        source, landing = ((send_x, recv_x), (send_y, recv_y))[t // 2]
         return pltpu.make_async_remote_copy(
-            src_ref=send_x.at[side], dst_ref=recv_x.at[side],
-            send_sem=send_sem.at[side], recv_sem=recv_sem.at[side],
-            device_id=targets[side], device_id_type=pl.DeviceIdType.MESH,
+            src_ref=source.at[t % 2], dst_ref=landing.at[t % 2],
+            send_sem=send_sem.at[t], recv_sem=recv_sem.at[t],
+            device_id=targets[t], device_id_type=pl.DeviceIdType.MESH,
         )
 
-    def send_y_copy(side, g):
-        return pltpu.make_async_remote_copy(
-            src_ref=send_y.at[side, g], dst_ref=recv_y.at[side, g],
-            send_sem=send_y_sem.at[side, g], recv_sem=recv_y_sem.at[side, g],
-            device_id=targets[2 + side], device_id_type=pl.DeviceIdType.MESH,
-        )
+    def send_sums():
+        @pl.when(first)
+        def _():
+            pl.semaphore_wait(barrier, 3)
+
+        @pl.when(jnp.logical_not(first))
+        def _():
+            pl.semaphore_wait(barrier, 4)
+
+        for t in range(3):
+            sum_copy(t).start()
+
+        @pl.when(jnp.logical_not(first))
+        def _():
+            sum_copy(3).start()
 
     consts[0].wait()
 
@@ -191,10 +210,6 @@
                 row = (c * 3 + 2) * half + k
                 send_x[0, h, row : row + 1] = bottom[EDGE - 1 :]
                 send_x[1, h, row : row + 1] = top[:1]
-
-    pl.semaphore_wait(barrier, 4)
-    for side in range(2):
-        send_x_copy(side).start()
 
     consts[1].wait()
 
@@ -218,7 +233,6 @@
                         send_y[1, g, row : row + 1] = sums[4 + q : 5 + q, j * n : (j + 1) * n]
         for side in range(2):
             send_y[side, g, 9 * GROUP :] = jnp.zeros((4, n), jnp.float32)
-            send_y_copy(side, g).start()
 
     lane = lax.broadcasted_iota(jnp.int32, (n, n), 1)
     consts[4].wait()
@@ -229,6 +243,10 @@
 
     @pl.loop(0, groups)
     def _(g):
+        @pl.when(g == sending_step)
+        def _():
+            send_sums()
+
         leaf_copy(g).wait()
         for k in range(0, GROUP, 2):
             z = (g * GROUP + k, g * GROUP + k + 1)
@@ -246,6 +264,10 @@
                     curvature = both[:, 1, :, j * n : (j + 1) * n].reshape(n, n)
                     tend[c, z[j]] = curvature - vel[0, z[j]] * gradient - drag[j] * vel[c, z[j]]
 
+    @pl.when(sending_step == groups)
+    def _():
+        send_sums()
+
     consts[3].wait()
 
     @pl.loop(0, groups)
@@ -259,14 +281,17 @@
                 curvature = both[c * n : (c + 1) * n, n:]
                 tend[c, z] += curvature - vel[1, z] * gradient
 
-    @pl.loop(0, groups)
-    def _(g):
-        for side in range(2):
-            send_y_copy(side, g).wait()
-
-    for side in range(2):
-        send_x_copy(side).wait()
     consts[5].wait()
+    sum_copy(2).wait_recv()
+
+    @pl.when(first)
+    def _():
+        sum_copy(3).start()
+
+    for t in (3, 0, 1):
+        sum_copy(t).wait_recv()
+    for t in range(4):
+        sum_copy(t).wait_send()
 
 
 def second_kernel(groups, vel, tend, recv_x, recv_y, spread_y, edge_x, out_hbm, result, out_sem):
@@ -345,7 +370,7 @@
             pltpu.VMEM(along_y.shape, BF16),
             pltpu.VMEM(sums_y.shape, BF16),
             pltpu.SMEM(drag_table.shape, jnp.float32),
-            dma((3, groups)), dma((groups,)), dma((6,)), dma((2,)), dma((2,)), dma((2, groups)), dma((2, groups)),
+            dma((3, groups)), dma((groups,)), dma((6,)), dma((4,)), dma((4,)),
         ],
         compiler_params=pltpu.CompilerParams(
             collective_id=0, has_side_effects=True, vmem_limit_bytes=40 * 1024 * 1024

time: 15.2 us -> 16 us (1.053)
  Pallas kernels: 15.1 us -> 15.9 us
    pallas_call x1, Pallas kernels: 12.8 us -> 13.7 us  [body(): pl.pallas_call(functools.partial(first_kernel, groups), out_shape=held, i...]
where the time goes in v4:
time: 16 us; the launch traced here: 15.9 us
  Pallas kernels  15.9 us (99%)
    pallas_call x1, Pallas kernels, body(): pl.pallas_call(functools.partial(first_kernel, groups), out_shape=held, i...  13.7 us
    pallas_call x1, Pallas kernels, body(): pl.pallas_call(functools.partial(second_kernel, groups), out_shape=jax.Sh...  2.27 us

profile of v4, /device:TPU:6, one launch (start us, length us, event | category | flops | bytes accessed | tf_op | source)
XLA Modules:
  0.0 15.9 jit_solution(3017424734743637607)
XLA Ops:
  0.0 13.7 %exchange_and_solve.1 = (f32[3,16,128,128]{3,2,1,0:T(8,128)S(1)}, f32[3,16,128,128]{3,2,1,0:T(8,128)S(1)}, f32[2,2,72,128]{3,2,1,0:T(8,128)S(1)}, f32[2,4,40,128...) custom-call(f32[3,16,128,128]{3,2,1,0:T(8,128)} %vel_hbm.1, s32[16,128,128]{2,1,0:T(8,128)} %leaf_hbm.1, ...), custom_call_target="tpu_custom_call" | custom-call | flops 4000000000 | bytes 5000000 | tf_op jit(solution)/shard_map/exchange_and_solve/pallas_call | solution.py:359
  13.7 2.3 %finish.1 = f32[3,16,128,128]{3,2,1,0:T(8,128)} custom-call(f32[3,16,128,128]{3,2,1,0:T(8,128)S(1)} %get-tuple-element.11.vel, f32[3,16,128,128]{3,2,1,0:T(8,128)S(1)} %get-tuple-element.12.tend, f32[2,2,72,128]{3,2,1,0:T(8,128)S(1)} %get-tuple-element.13.recv_x, f32[2,4,40,128]{3,2,1,0:T(8,128)S(1)} %get-tuple-element.14.recv_y, ...), custom_call_target="tpu_custom_call" | custom-call | flops 1000000000 | bytes 3000000 | tf_op jit(solution)/shard_map/finish/pallas_call | solution.py:381

commit v5 on v3

--- a/solution.py
+++ b/solution.py
@@ -107,7 +107,7 @@
     groups, vel_hbm, leaf_hbm, table_hbm, along_x_hbm, along_y_hbm, spread_y_hbm, sums_y_hbm, edge_x_hbm,
     vel, tend, recv_x, recv_y, spread_y, edge_x,
     parts, leaf, send_x, send_y, along_x, along_y, sums_y, table_ref,
-    vel_sem, leaf_sem, const_sem, send_sem, recv_sem, send_y_sem, recv_y_sem,
+    vel_sem, leaf_sem, const_sem, send_sem, recv_sem, send_y_sem, recv_y_sem, last_sem,
 ):
     n = CELLS
     half = 2 * GROUP
@@ -157,23 +157,60 @@
         {"gy": lax.rem(my + 1, ny)},
         {"gy": lax.rem(my + ny - 1, ny)},
     ]
+    first, last = my == 0, my == ny - 1
     barrier = pltpu.get_barrier_semaphore()
-    for target in targets:
+    for target in (targets[0], targets[1], targets[3]):
         pl.semaphore_signal(barrier, inc=1, device_id=target, device_id_type=pl.DeviceIdType.MESH)
 
-    def send_x_copy(side):
+    @pl.when(jnp.logical_not(last))
+    def _():
+        pl.semaphore_signal(barrier, inc=1, device_id=targets[2], device_id_type=pl.DeviceIdType.MESH)
+
+    late = jnp.logical_or(jnp.logical_and(last, mx != 0), mx == nx - 1)
+    punctual = jnp.logical_not(late)
+    sending_step = jnp.where(jnp.logical_and(mx == 0, jnp.logical_not(last)), groups, groups // 2)
+
+    def x_copy(side):
         return pltpu.make_async_remote_copy(
             src_ref=send_x.at[side], dst_ref=recv_x.at[side],
             send_sem=send_sem.at[side], recv_sem=recv_sem.at[side],
             device_id=targets[side], device_id_type=pl.DeviceIdType.MESH,
         )
 
-    def send_y_copy(side, g):
+    def y_copy(side, g):
         return pltpu.make_async_remote_copy(
             src_ref=send_y.at[side, g], dst_ref=recv_y.at[side, g],
             send_sem=send_y_sem.at[side, g], recv_sem=recv_y_sem.at[side, g],
             device_id=targets[2 + side], device_id_type=pl.DeviceIdType.MESH,
         )
+
+    def meet_and_send_x():
+        @pl.when(first)
+        def _():
+            pl.semaphore_wait(barrier, 3)
+
+        @pl.when(jnp.logical_not(first))
+        def _():
+            pl.semaphore_wait(barrier, 4)
+
+        @pl.when(last)
+        def _():
+            pl.semaphore_signal(last_sem, inc=1, device_id=targets[2], device_id_type=pl.DeviceIdType.MESH)
+
+        for side in range(2):
+            x_copy(side).start()
+
+    def send_y_group(g):
+        y_copy(0, g).start()
+
+        @pl.when(jnp.logical_not(first))
+        def _():
+            y_copy(1, g).start()
+
+    def meet_and_send():
+        meet_and_send_x()
+        for g in range(groups):
+            send_y_group(g)
 
     consts[0].wait()
 
@@ -192,9 +229,9 @@
                 send_x[0, h, row : row + 1] = bottom[EDGE - 1 :]
                 send_x[1, h, row : row + 1] = top[:1]
 
-    pl.semaphore_wait(barrier, 4)
-    for side in range(2):
-        send_x_copy(side).start()
+    @pl.when(late)
+    def _():
+        meet_and_send_x()
 
     consts[1].wait()
 
@@ -218,7 +255,10 @@
                         send_y[1, g, row : row + 1] = sums[4 + q : 5 + q, j * n : (j + 1) * n]
         for side in range(2):
             send_y[side, g, 9 * GROUP :] = jnp.zeros((4, n), jnp.float32)
-            send_y_copy(side, g).start()
+
+        @pl.when(late)
+        def _():
+            send_y_group(g)
 
     lane = lax.broadcasted_iota(jnp.int32, (n, n), 1)
     consts[4].wait()
@@ -229,6 +269,10 @@
 
     @pl.loop(0, groups)
     def _(g):
+        @pl.when(jnp.logical_and(punctual, g == sending_step))
+        def _():
+            meet_and_send()
+
         leaf_copy(g).wait()
         for k in range(0, GROUP, 2):
             z = (g * GROUP + k, g * GROUP + k + 1)
@@ -246,6 +290,10 @@
                     curvature = both[:, 1, :, j * n : (j + 1) * n].reshape(n, n)
                     tend[c, z[j]] = curvature - vel[0, z[j]] * gradient - drag[j] * vel[c, z[j]]
 
+    @pl.when(jnp.logical_and(punctual, sending_step == groups))
+    def _():
+        meet_and_send()
+
     consts[3].wait()
 
     @pl.loop(0, groups)
@@ -259,14 +307,23 @@
                 curvature = both[c * n : (c + 1) * n, n:]
                 tend[c, z] += curvature - vel[1, z] * gradient
 
-    @pl.loop(0, groups)
-    def _(g):
-        for side in range(2):
-            send_y_copy(side, g).wait()
+    consts[5].wait()
+
+    @pl.when(first)
+    def _():
+        pl.semaphore_wait(last_sem, 1)
+        for g in range(groups):
+            y_copy(1, g).start()
 
     for side in range(2):
-        send_x_copy(side).wait()
-    consts[5].wait()
+        for g in range(groups):
+            y_copy(side, g).wait_recv()
+    for side in range(2):
+        x_copy(side).wait_recv()
+    for side in range(2):
+        x_copy(side).wait_send()
+        for g in range(groups):
+            y_copy(side, g).wait_send()
 
 
 def second_kernel(groups, vel, tend, recv_x, recv_y, spread_y, edge_x, out_hbm, result, out_sem):
@@ -346,6 +403,7 @@
             pltpu.VMEM(sums_y.shape, BF16),
             pltpu.SMEM(drag_table.shape, jnp.float32),
             dma((3, groups)), dma((groups,)), dma((6,)), dma((2,)), dma((2,)), dma((2, groups)), dma((2, groups)),
+            pltpu.SemaphoreType.REGULAR,
         ],
         compiler_params=pltpu.CompilerParams(
             collective_id=0, has_side_effects=True, vmem_limit_bytes=40 * 1024 * 1024

time: 15.2 us -> 14.8 us (0.974)
  the two profiles are of different devices: /device:TPU:6 before, /device:TPU:16 now
where the time goes in v5:
time: 14.8 us; the launch traced here: 14.7 us
  Pallas kernels  14.7 us (99%)
    pallas_call x1, Pallas kernels, body(): pl.pallas_call(functools.partial(first_kernel, groups), out_shape=held, i...  12.4 us
    pallas_call x1, Pallas kernels, body(): pl.pallas_call(functools.partial(second_kernel, groups), out_shape=jax.Sh...  2.27 us

profile of v5, /device:TPU:16, one launch (start us, length us, event | category | flops | bytes accessed | tf_op | source)
XLA Modules:
  0.0 14.7 jit_solution(12759760372465192592)
XLA Ops:
  0.0 12.4 %exchange_and_solve.1 = (f32[3,16,128,128]{3,2,1,0:T(8,128)S(1)}, f32[3,16,128,128]{3,2,1,0:T(8,128)S(1)}, f32[2,2,72,128]{3,2,1,0:T(8,128)S(1)}, f32[2,4,40,128...) custom-call(f32[3,16,128,128]{3,2,1,0:T(8,128)} %vel_hbm.1, s32[16,128,128]{2,1,0:T(8,128)} %leaf_hbm.1, ...), custom_call_target="tpu_custom_call" | custom-call | flops 4000000000 | bytes 5000000 | tf_op jit(solution)/shard_map/exchange_and_solve/pallas_call | solution.py:391
  12.4 2.3 %finish.1 = f32[3,16,128,128]{3,2,1,0:T(8,128)} custom-call(f32[3,16,128,128]{3,2,1,0:T(8,128)S(1)} %get-tuple-element.11.vel, f32[3,16,128,128]{3,2,1,0:T(8,128)S(1)} %get-tuple-element.12.tend, f32[2,2,72,128]{3,2,1,0:T(8,128)S(1)} %get-tuple-element.13.recv_x, f32[2,4,40,128]{3,2,1,0:T(8,128)S(1)} %get-tuple-element.14.recv_y, ...), custom_call_target="tpu_custom_call" | custom-call | flops 1000000000 | bytes 3000000 | tf_op jit(solution)/shard_map/finish/pallas_call | solution.py:414

commit v6 on v5

--- a/solution.py
+++ b/solution.py
@@ -166,7 +166,9 @@
     def _():
         pl.semaphore_signal(barrier, inc=1, device_id=targets[2], device_id_type=pl.DeviceIdType.MESH)
 
-    late = jnp.logical_or(jnp.logical_and(last, mx != 0), mx == nx - 1)
+    late_x = mx == nx - 1
+    late_y = jnp.logical_and(last, mx != 0)
+    late = jnp.logical_or(late_x, late_y)
     punctual = jnp.logical_not(late)
     sending_step = jnp.where(jnp.logical_and(mx == 0, jnp.logical_not(last)), groups, groups // 2)
 
@@ -184,7 +186,7 @@
             device_id=targets[2 + side], device_id_type=pl.DeviceIdType.MESH,
         )
 
-    def meet_and_send_x():
+    def meet():
         @pl.when(first)
         def _():
             pl.semaphore_wait(barrier, 3)
@@ -197,20 +199,30 @@
         def _():
             pl.semaphore_signal(last_sem, inc=1, device_id=targets[2], device_id_type=pl.DeviceIdType.MESH)
 
+    def send_x_sums():
         for side in range(2):
             x_copy(side).start()
 
-    def send_y_group(g):
-        y_copy(0, g).start()
-
+    def send_y_back(g):
         @pl.when(jnp.logical_not(first))
         def _():
             y_copy(1, g).start()
 
-    def meet_and_send():
-        meet_and_send_x()
+    def send_rest():
+        @pl.when(punctual)
+        def _():
+            meet()
+
+        @pl.when(jnp.logical_not(late_x))
+        def _():
+            send_x_sums()
+
         for g in range(groups):
-            send_y_group(g)
+            @pl.when(jnp.logical_not(late_y))
+            def _():
+                y_copy(0, g).start()
+
+            send_y_back(g)
 
     consts[0].wait()
 
@@ -231,7 +243,11 @@
 
     @pl.when(late)
     def _():
-        meet_and_send_x()
+        meet()
+
+    @pl.when(late_x)
+    def _():
+        send_x_sums()
 
     consts[1].wait()
 
@@ -256,9 +272,9 @@
         for side in range(2):
             send_y[side, g, 9 * GROUP :] = jnp.zeros((4, n), jnp.float32)
 
-        @pl.when(late)
-        def _():
-            send_y_group(g)
+        @pl.when(late_y)
+        def _():
+            y_copy(0, g).start()
 
     lane = lax.broadcasted_iota(jnp.int32, (n, n), 1)
     consts[4].wait()
@@ -269,9 +285,9 @@
 
     @pl.loop(0, groups)
     def _(g):
-        @pl.when(jnp.logical_and(punctual, g == sending_step))
-        def _():
-            meet_and_send()
+        @pl.when(g == sending_step)
+        def _():
+            send_rest()
 
         leaf_copy(g).wait()
         for k in range(0, GROUP, 2):
@@ -290,9 +306,9 @@
                     curvature = both[:, 1, :, j * n : (j + 1) * n].reshape(n, n)
                     tend[c, z[j]] = curvature - vel[0, z[j]] * gradient - drag[j] * vel[c, z[j]]
 
-    @pl.when(jnp.logical_and(punctual, sending_step == groups))
+    @pl.when(sending_step == groups)
     def _():
-        meet_and_send()
+        send_rest()
 
     consts[3].wait()
 
@@ -335,33 +351,38 @@
         return pltpu.make_async_copy(result.at[:, z], out_hbm.at[:, z], out_sem.at[z])
 
     lane = lax.broadcasted_iota(jnp.int32, (n, 80), 1)
-    for g in range(groups):
-        spread = []
-        for c in range(3):
-            got = jnp.concatenate([recv_y[side, g, c * values : (c + 1) * values] for side in range(2)], axis=0)
-            high = got.astype(BF16).astype(jnp.float32)
-            low = (got - high).astype(BF16).astype(jnp.float32)
-            blank = jnp.zeros((8, n), jnp.float32)
-            spread.append(jnp.concatenate([high, low, high, blank], axis=0).T.astype(BF16))
-        for k in range(GROUP):
-            z = g * GROUP + k
-            mask = (lane % GROUP) == k
-            left = [jnp.where(mask, s, jnp.zeros_like(s)) for s in spread]
-            both = dot(jnp.concatenate(left, axis=0), spread_y[...])
+
+    @pl.loop(0, groups // 2)
+    def _(h):
+        for part in range(2):
+            g = h * 2 + part
+            spread = []
             for c in range(3):
-                gradient = both[c * n : (c + 1) * n, :n]
-                curvature = both[c * n : (c + 1) * n, n:]
-                values_z = tend[c, z] + curvature - vel[1, z] * gradient
-                ends = []
-                for side in range(2):
-                    h, at = g // 2, c * 3 * half + (g % 2) * GROUP + k
-                    s1, s2, s3 = (recv_x[side, h, at + q * half : at + q * half + 1] for q in range(3))
-                    gradient = edge_x[4 + 4 * side] * s1 + edge_x[6 + 4 * side] * s3
-                    curvature = edge_x[5 + 4 * side] * s2 + edge_x[7 + 4 * side] * s3
-                    rows = slice(side * (n - EDGE), side * (n - EDGE) + EDGE)
-                    ends.append(values_z[rows] + curvature - vel[0, z, rows] * gradient)
-                result[c, z] = jnp.concatenate([ends[0], values_z[EDGE : n - EDGE], ends[1]], axis=0)
-            out_copy(z).start()
+                got = jnp.concatenate([recv_y[side, g, c * values : (c + 1) * values] for side in range(2)], axis=0)
+                high = got.astype(BF16).astype(jnp.float32)
+                low = (got - high).astype(BF16).astype(jnp.float32)
+                blank = jnp.zeros((8, n), jnp.float32)
+                spread.append(jnp.concatenate([high, low, high, blank], axis=0).T.astype(BF16))
+            for k in range(GROUP):
+                z = g * GROUP + k
+                mask = (lane % GROUP) == k
+                left = [jnp.where(mask, s, jnp.zeros_like(s)) for s in spread]
+                both = dot(jnp.concatenate(left, axis=0), spread_y[...])
+                for c in range(3):
+                    gradient = both[c * n : (c + 1) * n, :n]
+                    curvature = both[c * n : (c + 1) * n, n:]
+                    values_z = tend[c, z] + curvature - vel[1, z] * gradient
+                    ends = []
+                    for side in range(2):
+                        at = c * 3 * half + part * GROUP + k
+                        s1, s2, s3 = (recv_x[side, h, at + q * half : at + q * half + 1] for q in range(3))
+                        gradient = edge_x[4 + 4 * side] * s1 + edge_x[6 + 4 * side] * s3
+                        curvature = edge_x[5 + 4 * side] * s2 + edge_x[7 + 4 * side] * s3
+                        rows = slice(side * (n - EDGE), side * (n - EDGE) + EDGE)
+                        ends.append(values_z[rows] + curvature - vel[0, z, rows] * gradient)
+                    result[c, z] = jnp.concatenate([ends[0], values_z[EDGE : n - EDGE], ends[1]], axis=0)
+                out_copy(z).start()
+
     for z in range(groups * GROUP):
         out_copy(z).wait()
 

time: 14.8 us -> 14.9 us (level)
  Pallas kernels: 14.7 us -> 14.9 us
where the time goes in v6:
time: 14.9 us
  Pallas kernels  14.9 us (100%)
    pallas_call x1, Pallas kernels, body(): pl.pallas_call(functools.partial(first_kernel, groups), out_shape=held, i...  12.4 us
    pallas_call x1, Pallas kernels, body(): pl.pallas_call(functools.partial(second_kernel, groups), out_shape=jax.Sh...  2.42 us

profile of v6, /device:TPU:16, one launch (start us, length us, event | category | flops | bytes accessed | tf_op | source)
XLA Modules:
  0.0 14.9 jit_solution(8244807701398101814)
XLA Ops:
  0.0 12.4 %exchange_and_solve.1 = (f32[3,16,128,128]{3,2,1,0:T(8,128)S(1)}, f32[3,16,128,128]{3,2,1,0:T(8,128)S(1)}, f32[2,2,72,128]{3,2,1,0:T(8,128)S(1)}, f32[2,4,40,128...) custom-call(f32[3,16,128,128]{3,2,1,0:T(8,128)} %vel_hbm.1, s32[16,128,128]{2,1,0:T(8,128)} %leaf_hbm.1, ...), custom_call_target="tpu_custom_call" | custom-call | flops 4000000000 | bytes 5000000 | tf_op jit(solution)/shard_map/exchange_and_solve/pallas_call | solution.py:412
  12.4 2.4 %finish.1 = f32[3,16,128,128]{3,2,1,0:T(8,128)} custom-call(f32[3,16,128,128]{3,2,1,0:T(8,128)S(1)} %get-tuple-element.11.vel, f32[3,16,128,128]{3,2,1,0:T(8,128)S(1)} %get-tuple-element.12.tend, f32[2,2,72,128]{3,2,1,0:T(8,128)S(1)} %get-tuple-element.13.recv_x, f32[2,4,40,128]{3,2,1,0:T(8,128)S(1)} %get-tuple-element.14.recv_y, ...), custom_call_target="tpu_custom_call" | custom-call | flops 1000000000 | bytes 3000000 | tf_op jit(solution)/shard_map/finish/pallas_call | solution.py:435

commit v7 on v5

--- a/solution.py
+++ b/solution.py
@@ -135,6 +135,23 @@
     def leaf_copy(g):
         return pltpu.make_async_copy(leaf_hbm.at[levels(g)], leaf.at[levels(g)], leaf_sem.at[g])
 
+    mx, my = lax.axis_index("gx"), lax.axis_index("gy")
+    nx, ny = lax.axis_size("gx"), lax.axis_size("gy")
+    targets = [
+        {"gx": lax.rem(mx + 1, nx)},
+        {"gx": lax.rem(mx + nx - 1, nx)},
+        {"gy": lax.rem(my + 1, ny)},
+        {"gy": lax.rem(my + ny - 1, ny)},
+    ]
+    first, last = my == 0, my == ny - 1
+    barrier = pltpu.get_barrier_semaphore()
+    for target in (targets[0], targets[1], targets[3]):
+        pl.semaphore_signal(barrier, inc=1, device_id=target, device_id_type=pl.DeviceIdType.MESH)
+
+    @pl.when(jnp.logical_not(last))
+    def _():
+        pl.semaphore_signal(barrier, inc=1, device_id=targets[2], device_id_type=pl.DeviceIdType.MESH)
+
     consts[0].start()
     for h in range(halves):
         for side in range(2):
@@ -149,24 +166,9 @@
     consts[3].start()
     consts[5].start()
 
-    mx, my = lax.axis_index("gx"), lax.axis_index("gy")
-    nx, ny = lax.axis_size("gx"), lax.axis_size("gy")
-    targets = [
-        {"gx": lax.rem(mx + 1, nx)},
-        {"gx": lax.rem(mx + nx - 1, nx)},
-        {"gy": lax.rem(my + 1, ny)},
-        {"gy": lax.rem(my + ny - 1, ny)},
-    ]
-    first, last = my == 0, my == ny - 1
-    barrier = pltpu.get_barrier_semaphore()
-    for target in (targets[0], targets[1], targets[3]):
-        pl.semaphore_signal(barrier, inc=1, device_id=target, device_id_type=pl.DeviceIdType.MESH)
-
-    @pl.when(jnp.logical_not(last))
-    def _():
-        pl.semaphore_signal(barrier, inc=1, device_id=targets[2], device_id_type=pl.DeviceIdType.MESH)
-
-    late = jnp.logical_or(jnp.logical_and(last, mx != 0), mx == nx - 1)
+    late_x = mx == nx - 1
+    late_y = jnp.logical_and(last, mx != 0)
+    late = jnp.logical_or(late_x, late_y)
     punctual = jnp.logical_not(late)
     sending_step = jnp.where(jnp.logical_and(mx == 0, jnp.logical_not(last)), groups, groups // 2)
 
@@ -184,7 +186,7 @@
             device_id=targets[2 + side], device_id_type=pl.DeviceIdType.MESH,
         )
 
-    def meet_and_send_x():
+    def meet():
         @pl.when(first)
         def _():
             pl.semaphore_wait(barrier, 3)
@@ -197,20 +199,30 @@
         def _():
             pl.semaphore_signal(last_sem, inc=1, device_id=targets[2], device_id_type=pl.DeviceIdType.MESH)
 
+    def send_x_sums():
         for side in range(2):
             x_copy(side).start()
 
-    def send_y_group(g):
-        y_copy(0, g).start()
-
+    def send_y_back(g):
         @pl.when(jnp.logical_not(first))
         def _():
             y_copy(1, g).start()
 
-    def meet_and_send():
-        meet_and_send_x()
+    def send_rest():
+        @pl.when(punctual)
+        def _():
+            meet()
+
+        @pl.when(jnp.logical_not(late_x))
+        def _():
+            send_x_sums()
+
         for g in range(groups):
-            send_y_group(g)
+            @pl.when(jnp.logical_not(late_y))
+            def _():
+                y_copy(0, g).start()
+
+            send_y_back(g)
 
     consts[0].wait()
 
@@ -231,7 +243,11 @@
 
     @pl.when(late)
     def _():
-        meet_and_send_x()
+        meet()
+
+    @pl.when(late_x)
+    def _():
+        send_x_sums()
 
     consts[1].wait()
 
@@ -256,9 +272,9 @@
         for side in range(2):
             send_y[side, g, 9 * GROUP :] = jnp.zeros((4, n), jnp.float32)
 
-        @pl.when(late)
-        def _():
-            send_y_group(g)
+        @pl.when(late_y)
+        def _():
+            y_copy(0, g).start()
 
     lane = lax.broadcasted_iota(jnp.int32, (n, n), 1)
     consts[4].wait()
@@ -269,9 +285,9 @@
 
     @pl.loop(0, groups)
     def _(g):
-        @pl.when(jnp.logical_and(punctual, g == sending_step))
-        def _():
-            meet_and_send()
+        @pl.when(g == sending_step)
+        def _():
+            send_rest()
 
         leaf_copy(g).wait()
         for k in range(0, GROUP, 2):
@@ -290,9 +306,9 @@
                     curvature = both[:, 1, :, j * n : (j + 1) * n].reshape(n, n)
                     tend[c, z[j]] = curvature - vel[0, z[j]] * gradient - drag[j] * vel[c, z[j]]
 
-    @pl.when(jnp.logical_and(punctual, sending_step == groups))
+    @pl.when(sending_step == groups)
     def _():
-        meet_and_send()
+        send_rest()
 
     consts[3].wait()
 
@@ -347,10 +363,10 @@
             z = g * GROUP + k
             mask = (lane % GROUP) == k
             left = [jnp.where(mask, s, jnp.zeros_like(s)) for s in spread]
-            both = dot(jnp.concatenate(left, axis=0), spread_y[...])
             for c in range(3):
-                gradient = both[c * n : (c + 1) * n, :n]
-                curvature = both[c * n : (c + 1) * n, n:]
+                both = dot(left[c], spread_y[...])
+                gradient = both[:, :n]
+                curvature = both[:, n:]
                 values_z = tend[c, z] + curvature - vel[1, z] * gradient
                 ends = []
                 for side in range(2):

time: 14.8 us -> 14.6 us (0.986)
  Pallas kernels: 14.7 us -> 14.5 us
    pallas_call x1, Pallas kernels: 2.27 us -> 2.08 us  [body(): pl.pallas_call(functools.partial(second_kernel, groups), out_shape=jax.Sh...]
where the time goes in v7:
time: 14.6 us; the launch traced here: 14.5 us
  Pallas kernels  14.5 us (99%)
    pallas_call x1, Pallas kernels, body(): pl.pallas_call(functools.partial(first_kernel, groups), out_shape=held, i...  12.4 us
    pallas_call x1, Pallas kernels, body(): pl.pallas_call(functools.partial(second_kernel, groups), out_shape=jax.Sh...  2.08 us

profile of v7, /device:TPU:16, one launch (start us, length us, event | category | flops | bytes accessed | tf_op | source)
XLA Modules:
  0.0 14.5 jit_solution(8032460147968758278)
XLA Ops:
  0.0 12.4 %exchange_and_solve.1 = (f32[3,16,128,128]{3,2,1,0:T(8,128)S(1)}, f32[3,16,128,128]{3,2,1,0:T(8,128)S(1)}, f32[2,2,72,128]{3,2,1,0:T(8,128)S(1)}, f32[2,4,40,128...) custom-call(f32[3,16,128,128]{3,2,1,0:T(8,128)} %vel_hbm.1, s32[16,128,128]{2,1,0:T(8,128)} %leaf_hbm.1, ...), custom_call_target="tpu_custom_call" | custom-call | flops 4000000000 | bytes 5000000 | tf_op jit(solution)/shard_map/exchange_and_solve/pallas_call | solution.py:407
  12.4 2.1 %finish.1 = f32[3,16,128,128]{3,2,1,0:T(8,128)} custom-call(f32[3,16,128,128]{3,2,1,0:T(8,128)S(1)} %get-tuple-element.11.vel, f32[3,16,128,128]{3,2,1,0:T(8,128)S(1)} %get-tuple-element.12.tend, f32[2,2,72,128]{3,2,1,0:T(8,128)S(1)} %get-tuple-element.13.recv_x, f32[2,4,40,128]{3,2,1,0:T(8,128)S(1)} %get-tuple-element.14.recv_y, ...), custom_call_target="tpu_custom_call" | custom-call | flops 1000000000 | bytes 3000000 | tf_op jit(solution)/shard_map/finish/pallas_call | solution.py:430

commit v8 on v7

--- a/solution.py
+++ b/solution.py
@@ -144,11 +144,13 @@
         {"gy": lax.rem(my + ny - 1, ny)},
     ]
     first, last = my == 0, my == ny - 1
+    told = mx == nx // 2
+    deferred = jnp.logical_and(first, jnp.logical_not(told))
     barrier = pltpu.get_barrier_semaphore()
     for target in (targets[0], targets[1], targets[3]):
         pl.semaphore_signal(barrier, inc=1, device_id=target, device_id_type=pl.DeviceIdType.MESH)
 
-    @pl.when(jnp.logical_not(last))
+    @pl.when(jnp.logical_or(jnp.logical_not(last), told))
     def _():
         pl.semaphore_signal(barrier, inc=1, device_id=targets[2], device_id_type=pl.DeviceIdType.MESH)
 
@@ -170,7 +172,8 @@
     late_y = jnp.logical_and(last, mx != 0)
     late = jnp.logical_or(late_x, late_y)
     punctual = jnp.logical_not(late)
-    sending_step = jnp.where(jnp.logical_and(mx == 0, jnp.logical_not(last)), groups, groups // 2)
+    slow = jnp.logical_or(jnp.logical_and(mx == 0, jnp.logical_not(last)), jnp.logical_and(first, told))
+    sending_step = jnp.where(slow, groups, groups // 2)
 
     def x_copy(side):
         return pltpu.make_async_remote_copy(
@@ -187,15 +190,15 @@
         )
 
     def meet():
-        @pl.when(first)
+        @pl.when(deferred)
         def _():
             pl.semaphore_wait(barrier, 3)
 
-        @pl.when(jnp.logical_not(first))
+        @pl.when(jnp.logical_not(deferred))
         def _():
             pl.semaphore_wait(barrier, 4)
 
-        @pl.when(last)
+        @pl.when(jnp.logical_and(last, jnp.logical_not(told)))
         def _():
             pl.semaphore_signal(last_sem, inc=1, device_id=targets[2], device_id_type=pl.DeviceIdType.MESH)
 
@@ -204,7 +207,7 @@
             x_copy(side).start()
 
     def send_y_back(g):
-        @pl.when(jnp.logical_not(first))
+        @pl.when(jnp.logical_not(deferred))
         def _():
             y_copy(1, g).start()
 
@@ -213,7 +216,7 @@
         def _():
             meet()
 
-        @pl.when(jnp.logical_not(late_x))
+        @pl.when(jnp.logical_not(jnp.logical_or(late_x, mx == 0)))
         def _():
             send_x_sums()
 
@@ -223,6 +226,10 @@
                 y_copy(0, g).start()
 
             send_y_back(g)
+
+        @pl.when(mx == 0)
+        def _():
+            send_x_sums()
 
     consts[0].wait()
 
@@ -241,12 +248,9 @@
                 send_x[0, h, row : row + 1] = bottom[EDGE - 1 :]
                 send_x[1, h, row : row + 1] = top[:1]
 
-    @pl.when(late)
+    @pl.when(late_x)
     def _():
         meet()
-
-    @pl.when(late_x)
-    def _():
         send_x_sums()
 
     consts[1].wait()
@@ -272,8 +276,13 @@
         for side in range(2):
             send_y[side, g, 9 * GROUP :] = jnp.zeros((4, n), jnp.float32)
 
-        @pl.when(late_y)
-        def _():
+    @pl.when(jnp.logical_and(late_y, jnp.logical_not(late_x)))
+    def _():
+        meet()
+
+    @pl.when(late_y)
+    def _():
+        for g in range(groups):
             y_copy(0, g).start()
 
     lane = lax.broadcasted_iota(jnp.int32, (n, n), 1)
@@ -325,7 +334,7 @@
 
     consts[5].wait()
 
-    @pl.when(first)
+    @pl.when(deferred)
     def _():
         pl.semaphore_wait(last_sem, 1)
         for g in range(groups):

time: 14.6 us -> 14.4 us (0.986)
  the two profiles are of different devices: /device:TPU:16 before, /device:TPU:6 now
where the time goes in v8:
time: 14.4 us
  Pallas kernels  14.4 us (100%)
    pallas_call x1, Pallas kernels, body(): pl.pallas_call(functools.partial(first_kernel, groups), out_shape=held, i...  12.3 us
    pallas_call x1, Pallas kernels, body(): pl.pallas_call(functools.partial(second_kernel, groups), out_shape=jax.Sh...  2.08 us

profile of v8, /device:TPU:6, one launch (start us, length us, event | category | flops | bytes accessed | tf_op | source)
XLA Modules:
  0.0 14.4 jit_solution(17142832268912195606)
XLA Ops:
  0.0 12.3 %exchange_and_solve.1 = (f32[3,16,128,128]{3,2,1,0:T(8,128)S(1)}, f32[3,16,128,128]{3,2,1,0:T(8,128)S(1)}, f32[2,2,72,128]{3,2,1,0:T(8,128)S(1)}, f32[2,4,40,128...) custom-call(f32[3,16,128,128]{3,2,1,0:T(8,128)} %vel_hbm.1, s32[16,128,128]{2,1,0:T(8,128)} %leaf_hbm.1, ...), custom_call_target="tpu_custom_call" | custom-call | flops 4000000000 | bytes 5000000 | tf_op jit(solution)/shard_map/exchange_and_solve/pallas_call | solution.py:416
  12.3 2.1 %finish.1 = f32[3,16,128,128]{3,2,1,0:T(8,128)} custom-call(f32[3,16,128,128]{3,2,1,0:T(8,128)S(1)} %get-tuple-element.11.vel, f32[3,16,128,128]{3,2,1,0:T(8,128)S(1)} %get-tuple-element.12.tend, f32[2,2,72,128]{3,2,1,0:T(8,128)S(1)} %get-tuple-element.13.recv_x, f32[2,4,40,128]{3,2,1,0:T(8,128)S(1)} %get-tuple-element.14.recv_y, ...), custom_call_target="tpu_custom_call" | custom-call | flops 1000000000 | bytes 3000000 | tf_op jit(solution)/shard_map/finish/pallas_call | solution.py:439

commit v9 on v8

--- a/solution.py
+++ b/solution.py
@@ -144,7 +144,8 @@
         {"gy": lax.rem(my + ny - 1, ny)},
     ]
     first, last = my == 0, my == ny - 1
-    told = mx == nx // 2
+    told = jnp.logical_or(mx == nx // 2, mx == nx // 2 - 1)
+    untold = jnp.logical_not(told)
     deferred = jnp.logical_and(first, jnp.logical_not(told))
     barrier = pltpu.get_barrier_semaphore()
     for target in (targets[0], targets[1], targets[3]):
@@ -219,6 +220,10 @@
         @pl.when(jnp.logical_not(jnp.logical_or(late_x, mx == 0)))
         def _():
             send_x_sums()
+
+        @pl.when(late_x)
+        def _():
+            x_copy(1).start()
 
         for g in range(groups):
             @pl.when(jnp.logical_not(late_y))
@@ -248,10 +253,13 @@
                 send_x[0, h, row : row + 1] = bottom[EDGE - 1 :]
                 send_x[1, h, row : row + 1] = top[:1]
 
+    @pl.when(jnp.logical_or(late_x, jnp.logical_and(late_y, untold)))
+    def _():
+        meet()
+
     @pl.when(late_x)
     def _():
-        meet()
-        send_x_sums()
+        x_copy(0).start()
 
     consts[1].wait()
 
@@ -276,12 +284,13 @@
         for side in range(2):
             send_y[side, g, 9 * GROUP :] = jnp.zeros((4, n), jnp.float32)
 
-    @pl.when(jnp.logical_and(late_y, jnp.logical_not(late_x)))
+        @pl.when(jnp.logical_and(late_y, jnp.logical_or(late_x, untold)))
+        def _():
+            y_copy(0, g).start()
+
+    @pl.when(jnp.logical_and(jnp.logical_and(late_y, told), jnp.logical_not(late_x)))
     def _():
         meet()
-
-    @pl.when(late_y)
-    def _():
         for g in range(groups):
             y_copy(0, g).start()
 

time: 14.4 us -> 14.4 us (level)
  no operation moved by 1% of the time
where the time goes in v9:
time: 14.4 us
  Pallas kernels  14.4 us (100%)
    pallas_call x1, Pallas kernels, body(): pl.pallas_call(functools.partial(first_kernel, groups), out_shape=held, i...  12.3 us
    pallas_call x1, Pallas kernels, body(): pl.pallas_call(functools.partial(second_kernel, groups), out_shape=jax.Sh...  2.08 us

profile of v9, /device:TPU:6, one launch (start us, length us, event | category | flops | bytes accessed | tf_op | source)
XLA Modules:
  0.0 14.4 jit_solution(17916031994305755293)
XLA Ops:
  0.0 12.3 %exchange_and_solve.1 = (f32[3,16,128,128]{3,2,1,0:T(8,128)S(1)}, f32[3,16,128,128]{3,2,1,0:T(8,128)S(1)}, f32[2,2,72,128]{3,2,1,0:T(8,128)S(1)}, f32[2,4,40,128...) custom-call(f32[3,16,128,128]{3,2,1,0:T(8,128)} %vel_hbm.1, s32[16,128,128]{2,1,0:T(8,128)} %leaf_hbm.1, ...), custom_call_target="tpu_custom_call" | custom-call | flops 4000000000 | bytes 5000000 | tf_op jit(solution)/shard_map/exchange_and_solve/pallas_call | solution.py:425
  12.3 2.1 %finish.1 = f32[3,16,128,128]{3,2,1,0:T(8,128)} custom-call(f32[3,16,128,128]{3,2,1,0:T(8,128)S(1)} %get-tuple-element.11.vel, f32[3,16,128,128]{3,2,1,0:T(8,128)S(1)} %get-tuple-element.12.tend, f32[2,2,72,128]{3,2,1,0:T(8,128)S(1)} %get-tuple-element.13.recv_x, f32[2,4,40,128]{3,2,1,0:T(8,128)S(1)} %get-tuple-element.14.recv_y, ...), custom_call_target="tpu_custom_call" | custom-call | flops 1000000000 | bytes 3000000 | tf_op jit(solution)/shard_map/finish/pallas_call | solution.py:448

commit v10 on v9

--- a/solution.py
+++ b/solution.py
@@ -107,7 +107,7 @@
     groups, vel_hbm, leaf_hbm, table_hbm, along_x_hbm, along_y_hbm, spread_y_hbm, sums_y_hbm, edge_x_hbm,
     vel, tend, recv_x, recv_y, spread_y, edge_x,
     parts, leaf, send_x, send_y, along_x, along_y, sums_y, table_ref,
-    vel_sem, leaf_sem, const_sem, send_sem, recv_sem, send_y_sem, recv_y_sem, last_sem,
+    vel_sem, leaf_sem, const_sem, send_sem, recv_sem, send_y_sem, recv_y_sem, last_sem, wrap_sem,
 ):
     n = CELLS
     half = 2 * GROUP
@@ -148,8 +148,14 @@
     untold = jnp.logical_not(told)
     deferred = jnp.logical_and(first, jnp.logical_not(told))
     barrier = pltpu.get_barrier_semaphore()
-    for target in (targets[0], targets[1], targets[3]):
+    apart = lax.rem(my, 4) == 2
+    owed = jnp.logical_and(mx == 0, apart)
+    for target in (targets[1], targets[3]):
         pl.semaphore_signal(barrier, inc=1, device_id=target, device_id_type=pl.DeviceIdType.MESH)
+
+    @pl.when(jnp.logical_not(jnp.logical_and(mx == nx - 1, apart)))
+    def _():
+        pl.semaphore_signal(barrier, inc=1, device_id=targets[0], device_id_type=pl.DeviceIdType.MESH)
 
     @pl.when(jnp.logical_or(jnp.logical_not(last), told))
     def _():
@@ -173,7 +179,7 @@
     late_y = jnp.logical_and(last, mx != 0)
     late = jnp.logical_or(late_x, late_y)
     punctual = jnp.logical_not(late)
-    slow = jnp.logical_or(jnp.logical_and(mx == 0, jnp.logical_not(last)), jnp.logical_and(first, told))
+    slow = jnp.logical_or(jnp.logical_and(mx == 0, jnp.logical_not(jnp.logical_or(last, apart))), jnp.logical_and(first, told))
     sending_step = jnp.where(slow, groups, groups // 2)
 
     def x_copy(side):
@@ -191,11 +197,11 @@
         )
 
     def meet():
-        @pl.when(deferred)
+        @pl.when(jnp.logical_or(deferred, owed))
         def _():
             pl.semaphore_wait(barrier, 3)
 
-        @pl.when(jnp.logical_not(deferred))
+        @pl.when(jnp.logical_not(jnp.logical_or(deferred, owed)))
         def _():
             pl.semaphore_wait(barrier, 4)
 
@@ -203,9 +209,20 @@
         def _():
             pl.semaphore_signal(last_sem, inc=1, device_id=targets[2], device_id_type=pl.DeviceIdType.MESH)
 
+        @pl.when(jnp.logical_and(mx == nx - 1, apart))
+        def _():
+            pl.semaphore_signal(wrap_sem, inc=1, device_id=targets[0], device_id_type=pl.DeviceIdType.MESH)
+
     def send_x_sums():
-        for side in range(2):
-            x_copy(side).start()
+        @pl.when(mx == nx // 2)
+        def _():
+            x_copy(1).start()
+
+        x_copy(0).start()
+
+        @pl.when(jnp.logical_not(jnp.logical_or(mx == nx // 2, owed)))
+        def _():
+            x_copy(1).start()
 
     def send_y_back(g):
         @pl.when(jnp.logical_not(deferred))
@@ -342,6 +359,11 @@
                 tend[c, z] += curvature - vel[1, z] * gradient
 
     consts[5].wait()
+
+    @pl.when(owed)
+    def _():
+        pl.semaphore_wait(wrap_sem, 1)
+        x_copy(1).start()
 
     @pl.when(deferred)
     def _():
@@ -437,7 +459,7 @@
             pltpu.VMEM(sums_y.shape, BF16),
             pltpu.SMEM(drag_table.shape, jnp.float32),
             dma((3, groups)), dma((groups,)), dma((6,)), dma((2,)), dma((2,)), dma((2, groups)), dma((2, groups)),
-            pltpu.SemaphoreType.REGULAR,
+            pltpu.SemaphoreType.REGULAR, pltpu.SemaphoreType.REGULAR,
         ],
         compiler_params=pltpu.CompilerParams(
             collective_id=0, has_side_effects=True, vmem_limit_bytes=40 * 1024 * 1024

time: 14.4 us -> 14.5 us (level)
  no operation moved by 1% of the time
where the time goes in v10:
time: 14.5 us; the launch traced here: 14.4 us
  Pallas kernels  14.4 us (99%)
    pallas_call x1, Pallas kernels, body(): pl.pallas_call(functools.partial(first_kernel, groups), out_shape=held, i...  12.3 us
    pallas_call x1, Pallas kernels, body(): pl.pallas_call(functools.partial(second_kernel, groups), out_shape=jax.Sh...  2.07 us

profile of v10, /device:TPU:6, one launch (start us, length us, event | category | flops | bytes accessed | tf_op | source)
XLA Modules:
  0.0 14.4 jit_solution(293050298084352907)
XLA Ops:
  0.0 12.3 %exchange_and_solve.1 = (f32[3,16,128,128]{3,2,1,0:T(8,128)S(1)}, f32[3,16,128,128]{3,2,1,0:T(8,128)S(1)}, f32[2,2,72,128]{3,2,1,0:T(8,128)S(1)}, f32[2,4,40,128...) custom-call(f32[3,16,128,128]{3,2,1,0:T(8,128)} %vel_hbm.1, s32[16,128,128]{2,1,0:T(8,128)} %leaf_hbm.1, ...), custom_call_target="tpu_custom_call" | custom-call | flops 4000000000 | bytes 5000000 | tf_op jit(solution)/shard_map/exchange_and_solve/pallas_call | solution.py:447
  12.3 2.1 %finish.1 = f32[3,16,128,128]{3,2,1,0:T(8,128)} custom-call(f32[3,16,128,128]{3,2,1,0:T(8,128)S(1)} %get-tuple-element.11.vel, f32[3,16,128,128]{3,2,1,0:T(8,128)S(1)} %get-tuple-element.12.tend, f32[2,2,72,128]{3,2,1,0:T(8,128)S(1)} %get-tuple-element.13.recv_x, f32[2,4,40,128]{3,2,1,0:T(8,128)S(1)} %get-tuple-element.14.recv_y, ...), custom_call_target="tpu_custom_call" | custom-call | flops 1000000000 | bytes 3000000 | tf_op jit(solution)/shard_map/finish/pallas_call | solution.py:470

commit v11 on v10

--- a/solution.py
+++ b/solution.py
@@ -182,12 +182,16 @@
     slow = jnp.logical_or(jnp.logical_and(mx == 0, jnp.logical_not(jnp.logical_or(last, apart))), jnp.logical_and(first, told))
     sending_step = jnp.where(slow, groups, groups // 2)
 
-    def x_copy(side):
+    def x_part(side, h):
         return pltpu.make_async_remote_copy(
-            src_ref=send_x.at[side], dst_ref=recv_x.at[side],
-            send_sem=send_sem.at[side], recv_sem=recv_sem.at[side],
+            src_ref=send_x.at[side, h], dst_ref=recv_x.at[side, h],
+            send_sem=send_sem.at[side, h], recv_sem=recv_sem.at[side, h],
             device_id=targets[side], device_id_type=pl.DeviceIdType.MESH,
         )
+
+    def start_x(side):
+        for h in range(halves):
+            x_part(side, h).start()
 
     def y_copy(side, g):
         return pltpu.make_async_remote_copy(
@@ -216,13 +220,13 @@
     def send_x_sums():
         @pl.when(mx == nx // 2)
         def _():
-            x_copy(1).start()
-
-        x_copy(0).start()
+            start_x(1)
+
+        start_x(0)
 
         @pl.when(jnp.logical_not(jnp.logical_or(mx == nx // 2, owed)))
         def _():
-            x_copy(1).start()
+            start_x(1)
 
     def send_y_back(g):
         @pl.when(jnp.logical_not(deferred))
@@ -240,7 +244,7 @@
 
         @pl.when(late_x)
         def _():
-            x_copy(1).start()
+            start_x(1)
 
         for g in range(groups):
             @pl.when(jnp.logical_not(late_y))
@@ -276,7 +280,7 @@
 
     @pl.when(late_x)
     def _():
-        x_copy(0).start()
+        start_x(0)
 
     consts[1].wait()
 
@@ -363,7 +367,7 @@
     @pl.when(owed)
     def _():
         pl.semaphore_wait(wrap_sem, 1)
-        x_copy(1).start()
+        start_x(1)
 
     @pl.when(deferred)
     def _():
@@ -375,9 +379,11 @@
         for g in range(groups):
             y_copy(side, g).wait_recv()
     for side in range(2):
-        x_copy(side).wait_recv()
+        for h in range(halves):
+            x_part(side, h).wait_recv()
     for side in range(2):
-        x_copy(side).wait_send()
+        for h in range(halves):
+            x_part(side, h).wait_send()
         for g in range(groups):
             y_copy(side, g).wait_send()
 
@@ -458,7 +464,7 @@
             pltpu.VMEM(along_y.shape, BF16),
             pltpu.VMEM(sums_y.shape, BF16),
             pltpu.SMEM(drag_table.shape, jnp.float32),
-            dma((3, groups)), dma((groups,)), dma((6,)), dma((2,)), dma((2,)), dma((2, groups)), dma((2, groups)),
+            dma((3, groups)), dma((groups,)), dma((6,)), dma((2, groups // 2)), dma((2, groups // 2)), dma((2, groups)), dma((2, groups)),
             pltpu.SemaphoreType.REGULAR, pltpu.SemaphoreType.REGULAR,
         ],
         compiler_params=pltpu.CompilerParams(

time: 14.5 us -> 14.5 us (level)
  no operation moved by 1% of the time
where the time goes in v11:
time: 14.5 us
  Pallas kernels  14.5 us (100%)
    pallas_call x1, Pallas kernels, body(): pl.pallas_call(functools.partial(first_kernel, groups), out_shape=held, i...  12.4 us
    pallas_call x1, Pallas kernels, body(): pl.pallas_call(functools.partial(second_kernel, groups), out_shape=jax.Sh...  2.07 us

profile of v11, /device:TPU:6, one launch (start us, length us, event | category | flops | bytes accessed | tf_op | source)
XLA Modules:
  0.0 14.5 jit_solution(1180290288236631933)
XLA Ops:
  0.0 12.4 %exchange_and_solve.1 = (f32[3,16,128,128]{3,2,1,0:T(8,128)S(1)}, f32[3,16,128,128]{3,2,1,0:T(8,128)S(1)}, f32[2,2,72,128]{3,2,1,0:T(8,128)S(1)}, f32[2,4,40,128...) custom-call(f32[3,16,128,128]{3,2,1,0:T(8,128)} %vel_hbm.1, s32[16,128,128]{2,1,0:T(8,128)} %leaf_hbm.1, ...), custom_call_target="tpu_custom_call" | custom-call | flops 4000000000 | bytes 5000000 | tf_op jit(solution)/shard_map/exchange_and_solve/pallas_call | solution.py:453
  12.4 2.1 %finish.1 = f32[3,16,128,128]{3,2,1,0:T(8,128)} custom-call(f32[3,16,128,128]{3,2,1,0:T(8,128)S(1)} %get-tuple-element.11.vel, f32[3,16,128,128]{3,2,1,0:T(8,128)S(1)} %get-tuple-element.12.tend, f32[2,2,72,128]{3,2,1,0:T(8,128)S(1)} %get-tuple-element.13.recv_x, f32[2,4,40,128]{3,2,1,0:T(8,128)S(1)} %get-tuple-element.14.recv_y, ...), custom_call_target="tpu_custom_call" | custom-call | flops 1000000000 | bytes 3000000 | tf_op jit(solution)/shard_map/finish/pallas_call | solution.py:476
